TPU v7x, 32 devices: a whole 2x2x4 slice. The times are simulated.
32 devices in a mesh: dp: 4 (over x, core), seq: 4 (over z), head: 2 (over y).
Axes of the slice: x: 2, y: 2, z: 4, core: 2. Of those that a mesh axis runs over, the one named last changes fastest.
Arguments:
- doc_ids: int32 [4096], P(('dp', 'seq')), parts along dimension 0, may hold values from 0 to 7, never falling along the last dimension, each value on 1 to 512 neighbouring positions
- light_q: bfloat16 [4096, 4096], P(('dp', 'seq'), 'head'), parts along dimension 0, may hold values from -0.59765625 to 0.59765625
- light_k: bfloat16 [4096, 4096], P(('dp', 'seq'), 'head'), parts along dimension 0, may hold values from -0.59765625 to 0.59765625
- light_v: bfloat16 [4096, 4096], P(('dp', 'seq'), 'head'), parts along dimension 0, may hold values from -6 to 6
- light_decay: float32 [32], P('head'), may hold values from 0 to 1
- light_grad_out: bfloat16 [4096, 4096], P(('dp', 'seq'), 'head'), parts along dimension 0, may hold values from -6 to 6
- soft_q: bfloat16 [4096, 4096], P(('dp', 'seq'), 'head'), parts along dimension 0, may hold values from -40 to 40
- soft_k: bfloat16 [4096, 4096], P(('dp', 'seq'), 'head'), parts along dimension 0, may hold values from -40 to 40
- soft_v: bfloat16 [4096, 4096], P(('dp', 'seq'), 'head'), parts along dimension 0, may hold values from -6 to 6
- soft_grad_out: bfloat16 [4096, 4096], P(('dp', 'seq'), 'head'), parts along dimension 0, may hold values from -6 to 6
Outputs:
- lightning_output: bfloat16 [4096, 4096], P(('dp', 'seq'), 'head'), parts along dimension 0
- lightning_query_gradient: bfloat16 [4096, 4096], P(('dp', 'seq'), 'head'), parts along dimension 0
- lightning_key_gradient: bfloat16 [4096, 4096], P(('dp', 'seq'), 'head'), parts along dimension 0
- lightning_value_gradient: bfloat16 [4096, 4096], P(('dp', 'seq'), 'head'), parts along dimension 0
- soft_out: bfloat16 [4096, 4096], P(('dp', 'seq'), 'head'), parts along dimension 0
- soft_dq: bfloat16 [4096, 4096], P(('dp', 'seq'), 'head'), parts along dimension 0
- soft_dk: bfloat16 [4096, 4096], P(('dp', 'seq'), 'head'), parts along dimension 0
- soft_dv: bfloat16 [4096, 4096], P(('dp', 'seq'), 'head'), parts along dimension 0
There are 4 independent parts, one for each index of `dp`. A program takes and returns all parts, laid end to end along the dimension named above; an argument that names none is the same for every part. Nothing has to cross between parts.
Inputs may be any that keep to these rules, and one draw needn't show every extreme that they name: `doc_ids`: document ids never fall along the sequence; each document holds at most 512 tokens, and one holds exactly that many.
All inputs are finite; a program needn't handle non-finite values.
Results may differ from a plain program's by a relative error of at most 0.02.
Values may be sent and summed in bfloat16 or wider, within the bound.
A program may use at most 128 MiB of HBM per device.

v0:
```python
import jax
import jax.numpy as jnp
from jax import lax
from jax.sharding import PartitionSpec as P

PRECISE = lax.Precision.HIGH


def entering(part, axis, combine, identity, reverse):
    count = lax.axis_size(axis)
    place = lax.axis_index(axis)
    ahead = count - 1 - place if reverse else place
    gathered = jax.tree.map(lambda a: lax.all_gather(a, axis), part)
    state = jax.tree.map(lambda a, e: jnp.zeros_like(a) + jnp.asarray(e, a.dtype), part, identity)

    def one(lap, state):
        source = count - 1 - lap if reverse else lap
        return combine(
            state, jax.tree.map(lambda a: lax.dynamic_index_in_dim(a, source, 0, False), gathered)
        )

    return lax.fori_loop(0, ahead, one, state)


def from_behind(value, axis, steps):
    count = lax.axis_size(axis)
    first, last = (max(0, -steps), min(count, count - steps))
    return lax.ppermute(value, axis, [(source, source + steps) for source in range(first, last)])


def join_forward(earlier, later):
    state_a, keep_a, head_a, tail_a = earlier
    state_b, keep_b, head_b, tail_b = later
    empty_a = tail_a < 0
    empty_b = tail_b < 0
    joined = (head_b == tail_b) & (head_b == tail_a)
    running_state = jnp.where(
        empty_b, state_a, jnp.where(joined, keep_b[:, None, None] * state_a + state_b, state_b)
    )
    return (
        running_state,
        keep_a * keep_b,
        jnp.where(empty_a, head_b, head_a),
        jnp.where(empty_b, tail_a, tail_b),
    )


def join_backward(earlier, later):
    state_h, keep_h, head_h, tail_h = earlier
    state_l, keep_l, head_l, tail_l = later
    empty_h = tail_h < 0
    empty_l = tail_l < 0
    joined = (head_l == tail_l) & (tail_l == head_h)
    running_state = jnp.where(
        empty_l, state_h, jnp.where(joined, keep_l[:, None, None] * state_h + state_l, state_l)
    )
    return (
        running_state,
        keep_h * keep_l,
        jnp.where(empty_l, head_h, head_l),
        jnp.where(empty_h, tail_l, tail_h),
    )


def mixed_result(form, left, right):
    return jnp.einsum(form, left, right, precision=PRECISE, preferred_element_type=jnp.float32)


def per_device(
    doc_ids,
    light_q,
    light_k,
    light_v,
    light_decay,
    light_grad_out,
    soft_q,
    soft_k,
    soft_v,
    soft_grad_out,
):
    tok_rows = light_q.shape[0]
    heads = light_decay.shape[0]
    width = light_q.shape[1] // heads
    shards = lax.axis_size("seq")
    total_rows = tok_rows * shards
    offset = lax.axis_index("seq") * tok_rows
    last_pos = offset + tok_rows - 1
    all_ids = lax.all_gather(doc_ids, "seq", axis=0, tiled=True)
    positions = offset + jnp.arange(tok_rows, dtype=jnp.int32)
    own_ids = doc_ids.astype(jnp.float32)
    within_segment_position = jnp.arange(tok_rows, dtype=jnp.int32)
    reach = min(shards - 1, (tok_rows + total_rows // 2 - 2) // tok_rows)
    query_half_rows = light_q.reshape(tok_rows, heads, width)
    key_half_rows = light_k.reshape(tok_rows, heads, width)
    value_half_rows = light_v.reshape(tok_rows, heads, width)
    backward_sequence_share = light_grad_out.reshape(tok_rows, heads, width)
    inside = (doc_ids[:, None] == doc_ids[None, :]) & (
        within_segment_position[None, :] <= within_segment_position[:, None]
    )
    distance = jnp.maximum(
        within_segment_position[:, None] - within_segment_position[None, :], 0
    ).astype(jnp.float32)
    weight = jnp.where(inside[None], jnp.exp(-light_decay[:, None, None] * distance[None]), 0.0)
    scores = (
        jnp.einsum(
            "thd,shd->hts", query_half_rows, key_half_rows, preferred_element_type=jnp.float32
        )
        * weight
    )
    lightning_output = mixed_result("hts,shd->thd", scores, value_half_rows)
    head_id = own_ids[0]
    tail_id = own_ids[-1]
    since_start = (within_segment_position + 1).astype(jnp.float32)
    until_end = (tok_rows - 1 - within_segment_position).astype(jnp.float32)
    start_decay = jnp.exp(-since_start[:, None] * light_decay[None, :])
    end_decay = jnp.exp(-until_end[:, None] * light_decay[None, :])
    offset_to_end = end_decay * (own_ids == tail_id)[:, None]
    running_state = mixed_result(
        "bto,btq->toq", key_half_rows * offset_to_end[:, :, None], value_half_rows
    )
    keep = jnp.exp(-light_decay * tok_rows)
    identity = (
        jnp.zeros_like(running_state),
        jnp.ones_like(keep),
        jnp.float32(-1.0),
        jnp.float32(-1.0),
    )
    inherited_memory_matrix, _, _, carried_id = entering(
        (running_state, keep, head_id, tail_id), "seq", join_forward, identity, False
    )
    distance_since_beginning = start_decay * (own_ids == carried_id)[:, None]
    lightning_output = lightning_output + mixed_result(
        "peb,ebi->pei",
        query_half_rows * distance_since_beginning[:, :, None],
        inherited_memory_matrix,
    )
    grad_scores = (
        jnp.einsum(
            "thv,shv->hts",
            backward_sequence_share,
            value_half_rows,
            preferred_element_type=jnp.float32,
        )
        * weight
    )
    lightning_query_gradient = mixed_result("hts,shk->thk", grad_scores, key_half_rows)
    lightning_query_gradient = lightning_query_gradient + mixed_result(
        "mcq,cxq->mcx",
        backward_sequence_share * distance_since_beginning[:, :, None],
        inherited_memory_matrix,
    )
    lightning_key_gradient = mixed_result("hts,thk->shk", grad_scores, query_half_rows)
    lightning_value_gradient = mixed_result("hts,thv->shv", scores, backward_sequence_share)
    opening_part = start_decay * (own_ids == head_id)[:, None]
    pending_state = mixed_result(
        "ejn,ejf->jnf", query_half_rows * opening_part[:, :, None], backward_sequence_share
    )
    returned_value, _, yielded_document_number, _ = entering(
        (pending_state, keep, head_id, tail_id), "seq", join_backward, identity, True
    )
    closing_part = (end_decay * (own_ids == yielded_document_number)[:, None])[:, :, None]
    lightning_key_gradient = (
        lightning_key_gradient
        + mixed_result("qpb,aqb->aqp", returned_value, value_half_rows) * closing_part
    )
    lightning_value_gradient = (
        lightning_value_gradient
        + mixed_result("dgp,zdg->zdp", returned_value, key_half_rows) * closing_part
    )
    scale = width ** (-0.5)
    soft_query = soft_q.reshape(tok_rows, heads, width)
    soft_grads = soft_grad_out.reshape(tok_rows, heads, width)
    soft_keys = soft_k.reshape(tok_rows, heads, width)
    soft_values = soft_v.reshape(tok_rows, heads, width)
    all_keys = jnp.zeros((total_rows, heads * width), jnp.bfloat16)
    all_values = jnp.zeros((total_rows, heads * width), jnp.bfloat16)
    for step in range(reach, 0, -1):
        far_keys, far_values = from_behind((soft_k, soft_v), "seq", step)
        place = jnp.maximum(offset - step * tok_rows, 0)
        all_keys = lax.dynamic_update_slice_in_dim(all_keys, far_keys, place, 0)
        all_values = lax.dynamic_update_slice_in_dim(all_values, far_values, place, 0)
    all_keys = lax.dynamic_update_slice_in_dim(all_keys, soft_k, offset, 0)
    all_values = lax.dynamic_update_slice_in_dim(all_values, soft_v, offset, 0)
    first_pos = jnp.sum(all_ids < doc_ids[0])
    doc_end = jnp.sum(all_ids <= doc_ids[-1]) - 1
    key_block = min(512, total_rows)
    key_count = total_rows // key_block
    block_order = jnp.arange(key_count, dtype=jnp.int32)

    def key_mask(start, count):
        key_pos = start + jnp.arange(count, dtype=jnp.int32)
        key_ids = lax.dynamic_slice_in_dim(all_ids, start, count)
        return (key_pos[None, :] <= positions[:, None]) & (key_ids[None, :] == doc_ids[:, None])

    def held_block(start):
        segment_attention_inputs = lax.dynamic_slice_in_dim(all_keys, start, key_block).reshape(
            key_block, heads, width
        )
        block_values = lax.dynamic_slice_in_dim(all_values, start, key_block).reshape(
            key_block, heads, width
        )
        return (segment_attention_inputs, block_values)

    def unused(start):
        return (start > last_pos) | (start + key_block - 1 < first_pos)

    def forward_block(carry, index):
        start = index * key_block

        def forward_update(inner):
            top, total, accum = inner
            segment_attention_inputs, block_values = held_block(start)
            allowed = key_mask(start, key_block)[None]
            logits = (
                jnp.einsum(
                    "thd,shd->hts",
                    soft_query,
                    segment_attention_inputs,
                    preferred_element_type=jnp.float32,
                )
                * scale
            )
            logits = jnp.where(allowed, logits, -1e30)
            fresh = jnp.maximum(top, jnp.max(logits, axis=2))
            factor = jnp.exp(top - fresh)
            expo = jnp.where(allowed, jnp.exp(logits - fresh[:, :, None]), 0.0)
            total = total * factor + jnp.sum(expo, axis=2)
            accum = accum * factor[:, :, None] + jnp.einsum(
                "hts,shd->htd",
                expo.astype(jnp.bfloat16),
                block_values,
                preferred_element_type=jnp.float32,
            )
            return (fresh, total, accum)

        return (lax.cond(unused(start), lambda inner: inner, forward_update, carry), None)

    start_carry = (
        jnp.full((heads, tok_rows), -1e30, jnp.float32),
        jnp.zeros((heads, tok_rows), jnp.float32),
        jnp.zeros((heads, tok_rows, width), jnp.float32),
    )
    (top, total, accum), _ = lax.scan(forward_block, start_carry, block_order)
    soft_out = jnp.transpose(accum / total[:, :, None], (1, 0, 2)).astype(jnp.bfloat16)
    lse = top + jnp.log(total)
    delta = jnp.sum(soft_grads.astype(jnp.float32) * soft_out.astype(jnp.float32), axis=2).T
    all_lse, all_delta = (
        lax.all_gather(lse, "seq", axis=1, tiled=True),
        lax.all_gather(delta, "seq", axis=1, tiled=True),
    )
    zero_rows = jnp.zeros((tok_rows, heads, width), jnp.float32)

    def query_block(carry, index):
        start = index * key_block

        def query_update(inner):
            segment_attention_inputs, block_values = held_block(start)
            allowed = key_mask(start, key_block)[None]
            logits = (
                jnp.einsum(
                    "thd,shd->hts",
                    soft_query,
                    segment_attention_inputs,
                    preferred_element_type=jnp.float32,
                )
                * scale
            )
            prob = jnp.where(
                allowed, jnp.exp(jnp.where(allowed, logits - lse[:, :, None], -1e30)), 0.0
            )
            dprob = jnp.einsum(
                "thd,shd->hts", soft_grads, block_values, preferred_element_type=jnp.float32
            )
            dlogit = (prob * (dprob - delta[:, :, None])).astype(jnp.bfloat16)
            return (
                inner
                + jnp.einsum(
                    "hts,shd->thd",
                    dlogit,
                    segment_attention_inputs,
                    preferred_element_type=jnp.float32,
                )
                * scale
            )

        return (lax.cond(unused(start), lambda inner: inner, query_update, carry), None)

    soft_dq, _ = lax.scan(query_block, zero_rows, block_order)

    def key_terms(piece_query, piece_grads, start, count):
        query_pos = start + jnp.arange(count, dtype=jnp.int32)
        query_ids = lax.dynamic_slice_in_dim(all_ids, start, count)
        lse_part = lax.dynamic_slice_in_dim(all_lse, start, count, 1)
        delta_part = lax.dynamic_slice_in_dim(all_delta, start, count, 1)
        allowed = (
            (positions[None, :] <= query_pos[:, None]) & (doc_ids[None, :] == query_ids[:, None])
        )[None]
        logits = (
            jnp.einsum("thd,shd->hts", piece_query, soft_keys, preferred_element_type=jnp.float32)
            * scale
        )
        prob = jnp.where(
            allowed, jnp.exp(jnp.where(allowed, logits - lse_part[:, :, None], -1e30)), 0.0
        )
        dv_part = jnp.einsum(
            "hts,thd->shd",
            prob.astype(jnp.bfloat16),
            piece_grads,
            preferred_element_type=jnp.float32,
        )
        dprob = jnp.einsum(
            "thd,shd->hts", piece_grads, soft_values, preferred_element_type=jnp.float32
        )
        dlogit = (prob * (dprob - delta_part[:, :, None])).astype(jnp.bfloat16)
        dk_part = (
            jnp.einsum("hts,thd->shd", dlogit, piece_query, preferred_element_type=jnp.float32)
            * scale
        )
        return (dk_part, dv_part)

    def key_piece(carry, piece_query, piece_grads, start):
        count = piece_query.shape[0]
        span_rows = count
        span_count = count // span_rows

        def span_step(inner, index):
            begin = index * span_rows
            query_part = piece_query.reshape(span_rows, heads, width)
            grads_part = piece_grads.reshape(span_rows, heads, width)
            query_start = start + begin

            def span_update(sums):
                dk_part, dv_part = key_terms(query_part, grads_part, query_start, span_rows)
                return (sums[0] + dk_part, sums[1] + dv_part)

            skipped = (query_start + span_rows - 1 < offset) | (query_start > doc_end)
            return (lax.cond(skipped, lambda sums: sums, span_update, inner), None)

        result, _ = lax.scan(span_step, carry, jnp.arange(span_count, dtype=jnp.int32))
        return result

    grad_pair = key_piece((zero_rows, zero_rows), soft_q, soft_grad_out, offset)
    for step in range(1, reach + 1):
        near_query, near_grads = from_behind((soft_q, soft_grad_out), "seq", -step)
        later_start = jnp.minimum(offset + step * tok_rows, total_rows - tok_rows)
        grad_pair = key_piece(grad_pair, near_query, near_grads, later_start)
    soft_dk, soft_dv = grad_pair
    flat = (tok_rows, heads * width)
    return (
        lightning_output.reshape(flat).astype(jnp.bfloat16),
        lightning_query_gradient.reshape(flat).astype(jnp.bfloat16),
        lightning_key_gradient.reshape(flat).astype(jnp.bfloat16),
        lightning_value_gradient.reshape(flat).astype(jnp.bfloat16),
        soft_out.reshape(flat),
        soft_dq.reshape(flat).astype(jnp.bfloat16),
        soft_dk.reshape(flat).astype(jnp.bfloat16),
        soft_dv.reshape(flat).astype(jnp.bfloat16),
    )


def solution(mesh):
    return jax.shard_map(
        per_device,
        mesh=mesh,
        in_specs=(
            P(("dp", "seq")),
            P(("dp", "seq"), "head"),
            P(("dp", "seq"), "head"),
            P(("dp", "seq"), "head"),
            P("head"),
            P(("dp", "seq"), "head"),
            P(("dp", "seq"), "head"),
            P(("dp", "seq"), "head"),
            P(("dp", "seq"), "head"),
            P(("dp", "seq"), "head"),
        ),
        out_specs=(
            P(("dp", "seq"), "head"),
            P(("dp", "seq"), "head"),
            P(("dp", "seq"), "head"),
            P(("dp", "seq"), "head"),
            P(("dp", "seq"), "head"),
            P(("dp", "seq"), "head"),
            P(("dp", "seq"), "head"),
            P(("dp", "seq"), "head"),
        ),
        check_vma=False,
    )
```

profile of v0, /device:TPU:28, one launch (start us, length us, event | category | flops | bytes accessed | tf_op | source)
XLA Modules:
  0.0 649.2 jit_solution(13244797654835317381)
XLA Ops:
  18.6 8.1 %all-reduce.3 = (f32[4]{0:T(128)S(1)}, f32[4]{0:T(128)S(1)}, f32[64]{0:T(128)S(1)}) all-reduce(f32[4]{0:T(128)S(1)} %get-tuple-element.1588, f32[4]{0:T(128)S(1)} %slice_dynamic-update-slice_fusion, f32[64]{0:T(128)S(1)} %get-tuple-element.1590), channel_id=1, replica_groups=mesh['dp'=4,'seq'=4,'head'=2] {'seq'}, use_global_device_ids=true, to_apply=%add | all-reduce | flops 72 | bytes 576
  31.7 64.7 %all-gather.9.cloned.1.call-done = f32[64,128,128]{2,1,0:T(8,128)} async-done(((f32[16,128,128]{2,1,0:T(8,128)}), f32[64,128,128]{2,1,0:T(8,128)}) %all-gather.9.cloned.1.call-update) | async-done | bytes 4194320 | tf_op jit(solution)/shard_map/all_gather | solution.py:13
  113.7 11.6 %collective-permute-start.7 = (bf16[256,2048]{0,1:T(8,128)(2,1)}, bf16[256,2048]{0,1:T(8,128)(2,1)}, u32[]{:S(2)}, u32[]{:S(2)}) collective-permute-start(bf16[256,2048]{0,1:T(8,128)(2,1)} %copy.223), channel_id=1, source_target_pairs={{2,0},{4,2},{6,4},{3,1},{5,3},{7,5},{10,8},{12,10},{14,12},{11,9},... | collective-permute-start | bytes 3145736 | tf_op jit(solution)/shard_map/ppermute | solution.py:28
  125.3 197.7 %all-gather.3 = s32[4,1,256]{2,1,0:T(1,128)S(1)} all-gather(s32[1,1,256]{2,1,0:T(1,128)S(1)} %bitcast.257), channel_id=1, replica_groups=mesh['dp'=4,'seq'=4,'head'=2] {'seq'}, dimensions={0}, use_global_device_ids=true | all-gather | bytes 5120 | tf_op jit(solution)/shard_map/all_gather | solution.py:88
  358.2 10.5 %dynamic_update_slice.21 = bf16[1024,2048]{0,1:T(8,128)(2,1)} dynamic-update-slice(bf16[1024,2048]{0,1:T(8,128)(2,1)} %broadcast.426.clone.1, bf16[256,2048]{0,1:T(8,128)(2,1)} %collective-permute-done.2, s32[]{:T(128)S(6)} %max.21, s32[]{:T(128)} %constant.244.clone.1) | dynamic-update-slice | bytes 2097156 | tf_op jit(solution)/shard_map/dynamic_update_slice | solution.py:181
  370.9 10.5 %dynamic_update_slice.22 = bf16[1024,2048]{0,1:T(8,128)(2,1)} dynamic-update-slice(bf16[1024,2048]{0,1:T(8,128)(2,1)} %dynamic_update_slice.21, bf16[256,2048]{0,1:T(8,128)(2,1)} %collective-permute-done.3, s32[]{:T(128)S(6)} %max.22, s32[]{:T(128)} %constant.244.clone.1) | dynamic-update-slice | bytes 2097156 | tf_op jit(solution)/shard_map/dynamic_update_slice | solution.py:181
  387.8 10.5 %dynamic_update_slice.18 = bf16[1024,2048]{0,1:T(8,128)(2,1)} dynamic-update-slice(bf16[1024,2048]{0,1:T(8,128)(2,1)} %broadcast.426.clone, bf16[256,2048]{0,1:T(8,128)(2,1)} %collective-permute-done, s32[]{:T(128)S(6)} %max.21, s32[]{:T(128)} %constant.244.clone.1) | dynamic-update-slice | bytes 2097156 | tf_op jit(solution)/shard_map/dynamic_update_slice | solution.py:180
  398.3 10.5 %dynamic_update_slice.19 = bf16[1024,2048]{0,1:T(8,128)(2,1)} dynamic-update-slice(bf16[1024,2048]{0,1:T(8,128)(2,1)} %dynamic_update_slice.18, bf16[256,2048]{0,1:T(8,128)(2,1)} %collective-permute-done.1, s32[]{:T(128)S(6)} %max.22, s32[]{:T(128)} %constant.244.clone.1) | dynamic-update-slice | bytes 2097156 | tf_op jit(solution)/shard_map/dynamic_update_slice | solution.py:180
  410.2 32.1 %while.86 = (s32[]{:T(128)}, f32[16,256]{1,0:T(8,128)S(1)}, f32[16,256]{1,0:T(8,128)S(1)}, f32[16,256,128]{2,1,0:T(8,128)S(1)}, s32[2]{0:T(128)S(1)}, /*index=5*...) while((s32[]{:T(128)}, f32[16,256]{1,0:T(8,128)S(1)}, ...), condition=%wide.region_10.11_spmd.clone, body=%wide.region_5.10_spmd.clone.sunk | while | flops 1102455552 | bytes 43793800 | solution.py:243
  412.0 14.3 %conditional.19 = (f32[16,256]{1,0:T(8,128)S(1)}, f32[16,256]{1,0:T(8,128)S(1)}, f32[16,256,128]{2,1,0:T(8,128)S(1)}) conditional(s32[]{:T(128)} %convert_element_type.282, (s32[]{:T(128)}, s32[]{:T(128)}, s32[1024]{0:T(1024)S(1)}, s32[256]{0:T(256)S(1)}, bf16[1024,2048]{0,1:T(8,128)(2,1)}, /*index=5*/bf16[256,16,128]{2,0,1:T(8,128)(2,1)}, ...), branch_computations={%region_6.8_spmd, %region_9.9_spmd} | conditional | flops 1102455552 | bytes 43759688 | solution.py:236
  428.2 14.0 %conditional.19 = (f32[16,256]{1,0:T(8,128)S(1)}, f32[16,256]{1,0:T(8,128)S(1)}, f32[16,256,128]{2,1,0:T(8,128)S(1)}) conditional(s32[]{:T(128)} %convert_element_type.282, (s32[]{:T(128)}, s32[]{:T(128)}, s32[1024]{0:T(1024)S(1)}, s32[256]{0:T(256)S(1)}, bf16[1024,2048]{0,1:T(8,128)(2,1)}, /*index=5*/bf16[256,16,128]{2,0,1:T(8,128)(2,1)}, ...), branch_computations={%region_6.8_spmd, %region_9.9_spmd} | conditional | flops 1102455552 | bytes 43759688 | solution.py:236
  449.0 48.5 %while.87 = (s32[]{:T(128)}, f32[256,16,128]{0,2,1:T(8,128)}, s32[2]{0:T(128)S(1)}, s32[]{:T(128)}, s32[]{:T(128)}, /*index=5*/bf16[1024,2048]{0,1:T(8,128)(2,1)...) while((s32[]{:T(128)}, f32[256,16,128]{0,2,1:T(8,128)}, ...), condition=%wide.region_15.16_spmd.clone, body=%wide.region_12.15_spmd.clone.sunk | while | flops 1626735360 | bytes 38059376 | solution.py:288
  451.1 22.3 %conditional.20 = (f32[256,16,128]{0,2,1:T(8,128)}) conditional(s32[]{:T(128)} %convert_element_type.283, (s32[]{:T(128)}, bf16[1024,2048]{0,1:T(8,128)(2,1)}, s32[]{:T(128)}, s32[1024]{0:T(1024)S(1)}, s32[256]{0:T(256)S(1)}, /*index=5*/bf16[256,16,128]{2,0,1:T(8,128)(2,1)}, f32[16,256]{1,0:T(8,128)S(1)}, bf16[1024,2048]{0,1:T(8,128)(2,1)}, ...), branch_computations={%region_13.13_spmd, %region_14.14_spmd} | conditional | flops 1626735360 | bytes 38058040 | solution.py:286
  463.5 9.9 %bitcast_add_fusion = f32[256,16,128]{0,2,1:T(8,128)} fusion(f32[256,16,128]{0,2,1:T(8,128)} %get-tuple-element.1024, bf16[512,16,128]{0,2,1:T(8,128)(2,1)S(1)} %bitcast.224, f32[16,512,256]{2,1,0:T(8,128)} %fusion.151, f32[16,256]{1,0:T(8,128)S(1)} %get-tuple-element.1034, f32[16,256]{1,0:T(8,128)S(1)} %get-tuple-element.1031, ...), kind=kOutput, calls=%fused_computation.34 | convolution fusion | flops 1089470464 | bytes 17989632 | tf_op jit(solution)/shard_map/while/body/eval_jaxpr/cond/branch_0_fun/hts,shd->thd/dot_general | solution.py:277
  475.4 22.0 %conditional.20 = (f32[256,16,128]{0,2,1:T(8,128)}) conditional(s32[]{:T(128)} %convert_element_type.283, (s32[]{:T(128)}, bf16[1024,2048]{0,1:T(8,128)(2,1)}, s32[]{:T(128)}, s32[1024]{0:T(1024)S(1)}, s32[256]{0:T(256)S(1)}, /*index=5*/bf16[256,16,128]{2,0,1:T(8,128)(2,1)}, f32[16,256]{1,0:T(8,128)S(1)}, bf16[1024,2048]{0,1:T(8,128)(2,1)}, ...), branch_computations={%region_13.13_spmd, %region_14.14_spmd} | conditional | flops 1626735360 | bytes 38058040 | solution.py:286
  487.5 9.9 %bitcast_add_fusion = f32[256,16,128]{0,2,1:T(8,128)} fusion(f32[256,16,128]{0,2,1:T(8,128)} %get-tuple-element.1024, bf16[512,16,128]{0,2,1:T(8,128)(2,1)S(1)} %bitcast.224, f32[16,512,256]{2,1,0:T(8,128)} %fusion.151, f32[16,256]{1,0:T(8,128)S(1)} %get-tuple-element.1034, f32[16,256]{1,0:T(8,128)S(1)} %get-tuple-element.1031, ...), kind=kOutput, calls=%fused_computation.34 | convolution fusion | flops 1089470464 | bytes 17989632 | tf_op jit(solution)/shard_map/while/body/eval_jaxpr/cond/branch_0_fun/hts,shd->thd/dot_general | solution.py:277
  502.1 13.1 %all_gather.46 = f32[16,1024]{1,0:T(8,128)S(1)} all-gather(f32[16,256]{1,0:T(8,128)S(1)} %get-tuple-element.2077), channel_id=1, replica_groups=mesh['dp'=4,'seq'=4,'head'=2] {'seq'}, dimensions={1}, use_global_device_ids=true | all-gather | bytes 81920 | tf_op jit(solution)/shard_map/all_gather | solution.py:248
  515.2 16.0 %all_gather.47 = f32[16,1024]{0,1:T(8,128)} all-gather(f32[16,256]{0,1:T(8,128)S(1)} %bitcast.256), channel_id=1, replica_groups=mesh['dp'=4,'seq'=4,'head'=2] {'seq'}, dimensions={1}, use_global_device_ids=true | all-gather | bytes 81920 | tf_op jit(solution)/shard_map/all_gather | solution.py:249
  533.0 20.6 %conditional.12 = (f32[256,16,128]{2,0,1:T(8,128)S(1)}, f32[256,16,128]{2,0,1:T(8,128)}) conditional(s32[]{:T(128)} %convert_element_type.199, (s32[256]{0:T(256)S(1)}, s32[]{:T(128)}, s32[256]{0:T(256)S(1)}, s32[1024]{0:T(1024)S(1)}, bf16[256,16,128]{0,2,1:T(8,128)(2,1)}, /*index=5*/bf16[256,16,128]{0,2,1:T(8,128)(2,1)}, ...), branch_computations={%region_17.18_spmd, %region_18.19_spmd} | conditional | flops 1088094464 | bytes 40295512 | solution.py:337
  553.7 15.8 %conditional.13 = ((f32[256,16,128]{2,0,1:T(8,128)S(1)}, f32[256,16,128]{2,0,1:T(8,128)})) conditional(s32[]{:T(128)} %convert_element_type.198, (s32[256]{0:T(256)S(1)}, s32[]{:T(128)}, s32[256]{0:T(256)S(1)}, s32[1024]{0:T(1024)S(1)}, bf16[256,16,128]{0,2,1:T(8,128)(2,1)}, /*index=5*/bf16[256,16,128]{0,2,1:T(8,128)(2,1)}, ...), branch_computations={%region_19.20_spmd, %region_20.21_spmd} | conditional | flops 1088094464 | bytes 61267096 | solution.py:337
  562.7 6.7 %bitcast_add_fusion.4 = f32[256,16,128]{2,0,1:T(8,128)S(1)} fusion(f32[256,16,128]{2,0,1:T(8,128)S(1)} %get-tuple-element.1061, bf16[256,16,128]{0,2,1:T(8,128)(2,1)} %get-tuple-element.1434, f32[16,256,256]{2,1,0:T(8,128)} %copy-done.16, bf16[256,16,128]{0,2,1:T(8,128)(2,1)} %get-tuple-element.1437, bf16[256,16,128]{0,2,1:T(8,128)(2,1)} %get-tuple-element.1438, ...), kind=kOutput, calls=%fused_computation.69 | convolution fusion | flops 545259520 | bytes 11632640 | tf_op jit(solution)/shard_map/while/body/eval_jaxpr/cond/branch_0_fun/hts,thd->shd/dot_general | solution.py:316
  570.8 26.9 %conditional.14 = (bf16[256,2048]{1,0:T(8,128)(2,1)}, bf16[256,2048]{1,0:T(8,128)(2,1)}) conditional(s32[]{:T(128)} %convert_element_type.197, (s32[256]{0:T(256)S(1)}, s32[]{:T(128)}, s32[256]{0:T(256)S(1)}, s32[1024]{0:T(1024)S(1)}, bf16[256,2048]{0,1:T(8,128)(2,1)}, /*index=5*/bf16[256,16,128]{0,2,1:T(8,128)(2,1)}, f32[16,1024]{1,0:T(8,128)S(1)}, ...), branch_computations={%region_21.22_spmd, %region_22.23_spmd} | conditional | flops 1089143040 | bytes 42392664
  579.7 6.7 %fusion.66 = bf16[256,16,128]{0,2,1:T(8,128)(2,1)} fusion(f32[256,16,128]{0,2,1:T(8,128)} %copy.250, bf16[256,16,128]{0,2,1:T(8,128)(2,1)} %bitcast.20, f32[16,256,256]{2,1,0:T(8,128)} %fusion.154, bf16[256,16,128]{0,2,1:T(8,128)(2,1)} %bitcast.21, bf16[256,16,128]{0,2,1:T(8,128)(2,1)S(1)} %copy-done.18, f32[16,256]{1,0:T(8,128)S(1)} %get-tuple-element.1575, ...), kind=kOutput, calls=%fused_computation.92 | convolution fusion | flops 545783808 | bytes 10584064 | tf_op jit(solution)/shard_map/while/body/eval_jaxpr/cond/branch_0_fun/hts,thd->shd/dot_general | solution.py:316
  609.2 20.3 %while.84 = (s32[]{:T(128)}, f32[16,128,128]{2,1,0:T(8,128)S(1)}, f32[]{:T(128)}, s32[]{:T(128)}, f32[4]{0:T(128)S(1)}, /*index=5*/f32[4]{0:T(128)S(1)}, f32[4,1...) while((s32[]{:T(128)}, f32[16,128,128]{2,1,0:T(8,128)S(1)}, ...), condition=%wide.region_1.2_spmd, body=%wide.region_0.1_spmd.sunk | while | flops 1048586 | bytes 3146148 | solution.py:22
  (235 shorter events, 230.1 us)
Async XLA Ops:
  7.2 91.4 %copy-start = (bf16[256,2048]{1,0:T(8,128)(2,1)S(1)}, bf16[256,2048]{1,0:T(8,128)(2,1)}, u32[]{:S(2)}) copy-start(bf16[256,2048]{1,0:T(8,128)(2,1)} %param.31) | copy-start | bytes 3145732
  7.2 8.0 %copy-start.23 = (f32[16]{0:T(128)S(1)}, f32[16]{0:T(128)}, u32[]{:S(2)}) copy-start(f32[16]{0:T(128)} %param.32) | copy-start | bytes 196
  7.2 89.2 %all-gather.9.cloned.1.call-start = ((), (), s32[]{:S(2)}) async-start(), calls=%async_computation.1 | async-start | bytes 5242880 | tf_op jit(solution)/shard_map/all_gather | solution.py:13
  7.3 9.8 %copy-start.25 = (f32[256]{0:T(256)}, f32[256]{0:T(256)S(1)}, u32[]{:S(2)}) copy-start(f32[256]{0:T(256)S(1)} %convert_negate_fusion) | copy-start | bytes 3076
  13.3 315.1 %copy-start.5 = (bf16[256,2048]{0,1:T(8,128)(2,1)}, bf16[256,2048]{0,1:T(8,128)(2,1)S(1)}, u32[]{:S(2)}) copy-start(bf16[256,2048]{0,1:T(8,128)(2,1)S(1)} %copy.297) | copy-start | bytes 3145732
  15.2 16.5 %copy-start.7 = (bf16[256,2048]{0,1:T(8,128)(2,1)}, bf16[256,2048]{0,1:T(8,128)(2,1)S(1)}, u32[]{:S(2)}) copy-start(bf16[256,2048]{0,1:T(8,128)(2,1)S(1)} %copy.298) | copy-start | bytes 3145732
  17.0 592.0 %all-gather.7.cloned.1.call-start = ((), (), s32[]{:S(2)}) async-start(), calls=%async_computation | async-start | bytes 5242880 | tf_op jit(solution)/shard_map/all_gather | solution.py:13
  96.6 12.1 %copy-start.1 = (f32[16,128,128]{2,1,0:T(8,128)}, f32[16,128,128]{2,1,0:T(8,128)S(1)}, u32[]{:S(2)}) copy-start(f32[16,128,128]{2,1,0:T(8,128)S(1)} %get-tuple-element.1111) | copy-start | bytes 3145732
  103.8 249.1 %collective-permute-start.2 = (bf16[256,2048]{0,1:T(8,128)(2,1)}, bf16[256,2048]{0,1:T(8,128)(2,1)}, u32[]{:S(2)}, u32[]{:S(2)}) collective-permute-start(bf16[256,2048]{0,1:T(8,128)(2,1)} %copy.218), channel_id=1, source_target_pairs={{0,4},{2,6},{1,5},{3,7},{8,12},{10,14},{9,13},{11,15},{16,20},{18,... | collective-permute-start | bytes 3145736 | tf_op jit(solution)/shard_map/ppermute | solution.py:28
  105.1 263.6 %collective-permute-start.3 = (bf16[256,2048]{0,1:T(8,128)(2,1)}, bf16[256,2048]{0,1:T(8,128)(2,1)}, u32[]{:S(2)}, u32[]{:S(2)}) collective-permute-start(bf16[256,2048]{0,1:T(8,128)(2,1)} %copy.218), channel_id=1, source_target_pairs={{0,2},{2,4},{4,6},{1,3},{3,5},{5,7},{8,10},{10,12},{12,14},{9,11},... | collective-permute-start | bytes 3145736 | tf_op jit(solution)/shard_map/ppermute | solution.py:28
  108.7 272.8 %collective-permute-start = (bf16[256,2048]{0,1:T(8,128)(2,1)}, bf16[256,2048]{0,1:T(8,128)(2,1)}, u32[]{:S(2)}, u32[]{:S(2)}) collective-permute-start(bf16[256,2048]{0,1:T(8,128)(2,1)} %copy.214), channel_id=1, source_target_pairs={{0,4},{2,6},{1,5},{3,7},{8,12},{10,14},{9,13},{11,15},{16,20},{18,... | collective-permute-start | bytes 3145736 | tf_op jit(solution)/shard_map/ppermute | solution.py:28
  110.0 215.7 %copy-start.10 = (bf16[256,2048]{1,0:T(8,128)(2,1)S(1)}, bf16[256,2048]{1,0:T(8,128)(2,1)}, u32[]{:S(2)}) copy-start(bf16[256,2048]{1,0:T(8,128)(2,1)} %param.30) | copy-start | bytes 3145732
  110.0 288.3 %collective-permute-start.1 = (bf16[256,2048]{0,1:T(8,128)(2,1)}, bf16[256,2048]{0,1:T(8,128)(2,1)}, u32[]{:S(2)}, u32[]{:S(2)}) collective-permute-start(bf16[256,2048]{0,1:T(8,128)(2,1)} %copy.214), channel_id=1, source_target_pairs={{0,2},{2,4},{4,6},{1,3},{3,5},{5,7},{8,10},{10,12},{12,14},{9,11},... | collective-permute-start | bytes 3145736 | tf_op jit(solution)/shard_map/ppermute | solution.py:28
  113.7 439.9 %collective-permute-start.7 = (bf16[256,2048]{0,1:T(8,128)(2,1)}, bf16[256,2048]{0,1:T(8,128)(2,1)}, u32[]{:S(2)}, u32[]{:S(2)}) collective-permute-start(bf16[256,2048]{0,1:T(8,128)(2,1)} %copy.223), channel_id=1, source_target_pairs={{2,0},{4,2},{6,4},{3,1},{5,3},{7,5},{10,8},{12,10},{14,12},{11,9},... | collective-permute-start | bytes 3145736 | tf_op jit(solution)/shard_map/ppermute | solution.py:28
  335.2 8.6 %copy-start.8 = (bf16[256,2048]{0,1:T(8,128)(2,1)S(1)}, bf16[256,2048]{0,1:T(8,128)(2,1)}, u32[]{:S(2)}) copy-start(bf16[256,2048]{0,1:T(8,128)(2,1)} %copy-done.7) | copy-start | bytes 3145732
  352.9 31.3 %copy-start.17 = (bf16[256,2048]{0,1:T(8,128)(2,1)S(1)}, bf16[256,2048]{0,1:T(8,128)(2,1)}, u32[]{:S(2)}) copy-start(bf16[256,2048]{0,1:T(8,128)(2,1)} %copy.218) | copy-start | bytes 3145732
  352.9 200.8 %collective-permute-start.6 = (bf16[256,2048]{0,1:T(8,128)(2,1)}, bf16[256,2048]{0,1:T(8,128)(2,1)}, u32[]{:S(2)}, u32[]{:S(2)}) collective-permute-start(bf16[256,2048]{0,1:T(8,128)(2,1)} %copy.217), channel_id=1, source_target_pairs={{2,0},{4,2},{6,4},{3,1},{5,3},{7,5},{10,8},{12,10},{14,12},{11,9},... | collective-permute-start | bytes 3145736 | tf_op jit(solution)/shard_map/ppermute | solution.py:28
  368.7 200.8 %collective-permute-start.5 = (bf16[256,2048]{0,1:T(8,128)(2,1)}, bf16[256,2048]{0,1:T(8,128)(2,1)}, u32[]{:S(2)}, u32[]{:S(2)}) collective-permute-start(bf16[256,2048]{0,1:T(8,128)(2,1)} %copy.223), channel_id=1, source_target_pairs={{4,0},{6,2},{5,1},{7,3},{12,8},{14,10},{13,9},{15,11},{20,16},{22,... | collective-permute-start | bytes 3145736 | tf_op jit(solution)/shard_map/ppermute | solution.py:28
  381.5 188.0 %collective-permute-start.4 = (bf16[256,2048]{0,1:T(8,128)(2,1)}, bf16[256,2048]{0,1:T(8,128)(2,1)}, u32[]{:S(2)}, u32[]{:S(2)}) collective-permute-start(bf16[256,2048]{0,1:T(8,128)(2,1)} %copy.217), channel_id=1, source_target_pairs={{4,0},{6,2},{5,1},{7,3},{12,8},{14,10},{13,9},{15,11},{20,16},{22,... | collective-permute-start | bytes 3145736 | tf_op jit(solution)/shard_map/ppermute | solution.py:28
  385.3 23.5 %copy-start.9 = (bf16[256,2048]{0,1:T(8,128)(2,1)S(1)}, bf16[256,2048]{0,1:T(8,128)(2,1)}, u32[]{:S(2)}) copy-start(bf16[256,2048]{0,1:T(8,128)(2,1)} %copy.214) | copy-start | bytes 3145732
  570.8 26.9 %copy-start.2 = (f32[16,128,128]{2,1,0:T(8,128)S(1)}, f32[16,128,128]{2,1,0:T(8,128)}, u32[]{:S(2)}) copy-start(f32[16,128,128]{2,1,0:T(8,128)} %copy-done.1) | copy-start | bytes 3145732
  570.8 26.9 %copy-start.22 = (f32[256,16]{0,1:T(8,128)S(1)}, f32[256,16]{0,1:T(8,128)}, u32[]{:S(2)}) copy-start(f32[256,16]{0,1:T(8,128)} %get-tuple-element.1581) | copy-start | bytes 49156
  609.2 20.4 %copy-start.24 = (f32[16]{0:T(128)S(1)}, f32[16]{0:T(128)}, u32[]{:S(2)}) copy-start(f32[16]{0:T(128)} %param.32) | copy-start | bytes 196
  609.2 20.4 %copy-start.26 = (f32[256]{0:T(256)S(1)}, f32[256]{0:T(256)}, u32[]{:S(2)}) copy-start(f32[256]{0:T(256)} %copy-done.25) | copy-start | bytes 3076
  (18 other events, 68.0 us)
Sparse Core Ops, SparseCore 0:
  17.1 79.2 all-gather.8
  101.7 171.7 all-gather.6
where the time goes:
time: 653 us; the launch traced here: 649 us
  blocking collectives  235 us (36%)
  local copies, waits for them, and re-layouts  141 us (22%)
  matrix products  130 us (20%)
  waiting for transfers between devices  64.8 us (10%)
  starting transfers between devices  24.7 us (4%)
  other arithmetic  20.8 us (3%)
  between operations  16.3 us (2%)
  loops' own time  16.2 us (2%)
    all_gather x1, blocking collectives, per_device(): all_ids = lax.all_gather(doc_ids, 'seq', axis=0, tiled=True)  198 us
    all_gather x2, waiting for transfers between devices, entering(): gathered = jax.tree.map(lambda a: lax.all_gather(a, axis), part)  64.7 us
    dot_general x10, matrix products, mixed_result(): jnp.einsum(form, left, right, precision=PRECISE, preferred_element_type=j...  35.1 us
    unnamed x72, local copies, waits for them, and re-layouts  29.7 us
    ppermute x8, starting transfers between devices, from_behind(): lax.ppermute(value, axis, [(source, source + steps) for source in range(f...  24.7 us
    dynamic_slice x4, local copies, waits for them, and re-layouts, held_block(): lax.dynamic_slice_in_dim(all_values, start, key_block)  21.9 us
    dynamic_update_slice x2, local copies, waits for them, and re-layouts, per_device(): lax.dynamic_update_slice_in_dim(all_values, far_values, place, 0)  21 us
    dynamic_update_slice x2, local copies, waits for them, and re-layouts, per_device(): all_keys = lax.dynamic_update_slice_in_dim(all_keys, far_keys, place, 0)  21 us
  transfers between devices with their start and end apart: 10, of which 1 were waited for; matrix products, arithmetic and copies ran while one was open for 39% of the time, Pallas kernels for 0%

commit v1 on v0

v1 whole, which is shorter than its diff:
```python
import functools
import math

import jax
import jax.numpy as jnp
from jax import lax
from jax.experimental import pallas as pl
from jax.experimental.pallas import tpu as pltpu
from jax.sharding import PartitionSpec as P

NEG = -1e30
F32 = jnp.float32
BF16 = jnp.bfloat16
VMEM_LIMIT = 50 * 1024 * 1024


def mm(a, b, ca, cb):
    return lax.dot_general(a, b, (((ca,), (cb,)), ((), ())), preferred_element_type=F32)


def shift(value, axis, steps):
    count = lax.axis_size(axis)
    first, last = (max(0, -steps), min(count, count - steps))
    return lax.ppermute(value, axis, [(source, source + steps) for source in range(first, last)])


def relay(value, axis, steps, reach):
    got = []
    for _ in range(reach):
        value = shift(value, axis, steps)
        got.append(value)
    return got


def state_kernel(hb, width, decay, ids_col, q, k, v, g, ahead, back):
    rows = q.shape[0]
    base = pl.program_id(0) * hb
    ids = ids_col[...]
    pos = lax.broadcasted_iota(jnp.int32, (rows, width), 0).astype(F32)
    head_on = jnp.where(ids == ids_col[0:1, :], 0.0, NEG)
    tail_on = jnp.where(ids == ids_col[rows - 1 : rows, :], 0.0, NEG)
    for h in range(hb):
        lam = decay[base + h]
        cols = slice(h * width, (h + 1) * width)
        to_end = jnp.exp(tail_on - lam * (rows - 1.0 - pos))
        since = jnp.exp(head_on - lam * (pos + 1.0))
        kd = (k[:, cols].astype(F32) * to_end).astype(BF16)
        qd = (q[:, cols].astype(F32) * since).astype(BF16)
        ahead[h] = mm(kd, v[:, cols], 0, 0).astype(BF16)
        back[h] = mm(qd, g[:, cols], 0, 0).astype(BF16)


def light_kernel(hb, width, reach, decay, coef_f, coef_b, ids_col, ids_row, q, k, v, g, *rest):
    states_f, states_b = rest[:reach], rest[reach : 2 * reach]
    out, dq, dk, dv, bias, dist = rest[2 * reach :]
    rows = q.shape[0]
    base = pl.program_id(0) * hb
    ids = ids_col[...]

    @pl.when(pl.program_id(0) == 0)
    def _():
        t = lax.broadcasted_iota(jnp.int32, (rows, rows), 0)
        s = lax.broadcasted_iota(jnp.int32, (rows, rows), 1)
        bias[...] = jnp.where((ids == ids_row[...]) & (s <= t), 0.0, NEG)
        dist[...] = jnp.maximum(t - s, 0).astype(F32)

    pos = lax.broadcasted_iota(jnp.int32, (rows, width), 0).astype(F32)
    head_on = jnp.where(ids == ids_col[0:1, :], 0.0, NEG)
    tail_on = jnp.where(ids == ids_col[rows - 1 : rows, :], 0.0, NEG)
    for h in range(hb):
        lam = decay[base + h]
        cols = slice(h * width, (h + 1) * width)
        qh, kh, vh, gh = q[:, cols], k[:, cols], v[:, cols], g[:, cols]
        state = coef_f[0, base + h] * states_f[0][h].astype(F32)
        later = coef_b[0, base + h] * states_b[0][h].astype(F32)
        for d in range(1, reach):
            state = state + coef_f[d, base + h] * states_f[d][h].astype(F32)
            later = later + coef_b[d, base + h] * states_b[d][h].astype(F32)
        state, later = state.astype(BF16), later.astype(BF16)
        to_end = jnp.exp(tail_on - lam * (rows - 1.0 - pos))
        since = jnp.exp(head_on - lam * (pos + 1.0))
        weight = jnp.exp(bias[...] - lam * dist[...])
        scores = (mm(qh, kh, 1, 1) * weight).astype(BF16)
        grads = (mm(gh, vh, 1, 1) * weight).astype(BF16)
        out[:, cols] = (mm(scores, vh, 1, 0) + mm(qh, state, 1, 0) * since).astype(BF16)
        dq[:, cols] = (mm(grads, kh, 1, 0) + mm(gh, state, 1, 1) * since).astype(BF16)
        dk[:, cols] = (mm(grads, qh, 0, 0) + mm(vh, later, 1, 1) * to_end).astype(BF16)
        dv[:, cols] = (mm(scores, gh, 0, 0) + mm(kh, later, 1, 0) * to_end).astype(BF16)


def query_kernel(hb, width, reach, fresh, ids_col, ids_row, q, g, k0, v0, *rest):
    far, rest = rest[:reach], rest[reach:]
    out, dq, stat, bias = rest if fresh else rest[2:]
    rows = q.shape[0]
    scale = width ** -0.5

    @pl.when(pl.program_id(0) == 0)
    def _():
        ids = ids_col[...]
        t = lax.broadcasted_iota(jnp.int32, (rows, rows), 0)
        s = lax.broadcasted_iota(jnp.int32, (rows, rows), 1)
        for d in range(reach + 1):
            same = ids == ids_row[:, d * rows : (d + 1) * rows]
            if d == 0:
                same = same & (s <= t)
            bias[d] = jnp.where(same, 0.0, NEG)

    lane = lax.broadcasted_iota(jnp.int32, (rows, width), 1)
    for h in range(hb):
        cols = slice(h * width, (h + 1) * width)
        qh, gh = q[:, cols], g[:, cols]
        keys = [k0[:, cols]] + [m[0, :, cols] for m in far]
        values = [v0[:, cols]] + [m[1, :, cols] for m in far]
        raw = [mm(qh, kh, 1, 1) + bias[d] for d, kh in enumerate(keys)]
        top = functools.reduce(jnp.maximum, raw).max(axis=1, keepdims=True)
        expo = [jnp.exp2((r - top) * (scale * math.log2(math.e))) for r in raw]
        total = functools.reduce(jnp.add, expo).sum(axis=1, keepdims=True)
        acc = functools.reduce(
            jnp.add, [mm(e.astype(BF16), vh, 1, 0) for e, vh in zip(expo, values)]
        )
        inv = 1.0 / total
        o16 = (acc * inv).astype(BF16)
        out[:, cols] = o16
        delta = (gh.astype(F32) * o16.astype(F32)).sum(axis=1, keepdims=True)
        lse = top + jnp.log(total) * (1.0 / scale)
        acc = None
        for e, kh, vh in zip(expo, keys, values):
            ds = ((e * inv) * (mm(gh, vh, 1, 1) - delta)).astype(BF16)
            part = mm(ds, kh, 1, 0)
            acc = part if acc is None else acc + part
        dq[:, cols] = (acc * scale).astype(BF16)
        stat[h] = jnp.where(lane == 0, lse, delta).T[0:2, :]


def key_kernel(hb, width, reach, fresh, ids_col, ids_row, k, v, q0, g0, stat0, *rest):
    far, stats, rest = rest[:reach], rest[reach : 2 * reach], rest[2 * reach :]
    dk, dv, bias = rest if fresh else rest[2:]
    rows = k.shape[0]
    scale = width ** -0.5

    @pl.when(pl.program_id(0) == 0)
    def _():
        ids = ids_col[...]
        s = lax.broadcasted_iota(jnp.int32, (rows, rows), 0)
        t = lax.broadcasted_iota(jnp.int32, (rows, rows), 1)
        for d in range(reach + 1):
            same = ids == ids_row[:, d * rows : (d + 1) * rows]
            if d == 0:
                same = same & (s <= t)
            bias[d] = jnp.where(same, 0.0, NEG)

    for h in range(hb):
        cols = slice(h * width, (h + 1) * width)
        kh, vh = k[:, cols], v[:, cols]
        dk_acc = dv_acc = None
        for d in range(reach + 1):
            qh = q0[:, cols] if d == 0 else far[d - 1][0, :, cols]
            gh = g0[:, cols] if d == 0 else far[d - 1][1, :, cols]
            st = stat0[h] if d == 0 else stats[d - 1][h]
            lse, delta = st[0:1, :], st[1:2, :]
            raw = mm(kh, qh, 1, 1) + bias[d]
            prob = jnp.exp2((raw - lse) * (scale * math.log2(math.e)))
            ds = (prob * (mm(vh, gh, 1, 1) - delta)).astype(BF16)
            dv_part = mm(prob.astype(BF16), gh, 1, 0)
            dk_part = mm(ds, qh, 1, 0)
            dk_acc = dk_part if dk_acc is None else dk_acc + dk_part
            dv_acc = dv_part if dv_acc is None else dv_acc + dv_part
        dk[:, cols] = (dk_acc * scale).astype(BF16)
        dv[:, cols] = dv_acc.astype(BF16)


def per_device(
    doc_ids,
    light_q,
    light_k,
    light_v,
    light_decay,
    light_grad_out,
    soft_q,
    soft_k,
    soft_v,
    soft_grad_out,
):
    rows, cols = light_q.shape
    heads = light_decay.shape[0]
    width = cols // heads
    shards = lax.axis_size("seq")
    total_rows = rows * shards
    reach = min(shards - 1, (rows + total_rows // 2 - 2) // rows)
    groups = 4 if heads % 4 == 0 else 1
    per_group = heads // groups
    hb = 2 if per_group % 2 == 0 else 1
    if reach > 2:
        hb = 1
    gw = per_group * width
    steps = per_group // hb
    bw = hb * width
    full = jax.ShapeDtypeStruct((rows, cols), BF16)
    params = pltpu.CompilerParams(vmem_limit_bytes=VMEM_LIMIT)
    smem = pl.BlockSpec(memory_space=pltpu.SMEM)

    def whole(shape):
        return pl.BlockSpec(shape, lambda i: (0,) * len(shape))

    ids = doc_ids + 1
    ids_before = relay(ids, "seq", 1, reach)
    ids_after = relay(ids, "seq", -1, reach)

    def cut(a, g):
        return a[:, g * gw : (g + 1) * gw]

    before, after = [], []
    for g in range(groups):
        before.append(relay(jnp.stack([cut(soft_k, g), cut(soft_v, g)]), "seq", 1, reach))
        after.append(relay(jnp.stack([cut(soft_q, g), cut(soft_grad_out, g)]), "seq", -1, reach))

    ids_col = ids[:, None]
    row_before = jnp.concatenate([ids] + ids_before)[None, :]
    row_after = jnp.concatenate([ids] + ids_after)[None, :]
    col_spec = whole((rows, 1))
    row_spec = whole((1, rows * (reach + 1)))

    lhb = hb
    lspec = pl.BlockSpec((rows, lhb * width), lambda i: (0, i))
    sspec = pl.BlockSpec((lhb, width, width), lambda i: (i, 0, 0))
    state_shape = jax.ShapeDtypeStruct((heads, width, width), BF16)
    state, pending = pl.pallas_call(
        functools.partial(state_kernel, lhb, width),
        grid=(heads // lhb,),
        in_specs=[smem, col_spec] + [lspec] * 4,
        out_specs=[sspec] * 2,
        out_shape=[state_shape] * 2,
        compiler_params=params,
        cost_estimate=pl.CostEstimate(
            flops=4 * rows * width * cols, bytes_accessed=10 * rows * cols, transcendentals=0
        ),
        name="light_states",
    )(light_decay, ids_col, light_q, light_k, light_v, light_grad_out)
    states_f = relay(state, "seq", 1, reach)
    states_b = relay(pending, "seq", -1, reach)
    lap = jnp.arange(reach, dtype=F32)[:, None]
    keep = jnp.exp(-light_decay[None, :] * (lap * rows))
    gate_f = jnp.stack([a[-1] == ids[0] for a in ids_before])
    gate_b = jnp.stack([a[0] == ids[-1] for a in ids_after])
    coef_f = jnp.where(gate_f[:, None], keep, 0.0)
    coef_b = jnp.where(gate_b[:, None], keep, 0.0)
    light = pl.pallas_call(
        functools.partial(light_kernel, lhb, width, reach),
        grid=(heads // lhb,),
        in_specs=[smem] * 3
        + [col_spec, whole((1, rows))]
        + [lspec] * 4
        + [sspec] * (2 * reach),
        out_specs=[lspec] * 4,
        out_shape=[full] * 4,
        scratch_shapes=[pltpu.VMEM((rows, rows), F32)] * 2,
        compiler_params=params,
        cost_estimate=pl.CostEstimate(
            flops=24 * rows * rows * cols, bytes_accessed=16 * rows * cols, transcendentals=0
        ),
        name="light",
    )(
        light_decay,
        coef_f,
        coef_b,
        ids_col,
        ids[None, :],
        light_q,
        light_k,
        light_v,
        light_grad_out,
        *states_f,
        *states_b,
    )

    bias = pltpu.VMEM((reach + 1, rows, rows), F32)
    far_spec = pl.BlockSpec((2, rows, bw), lambda i: (0, 0, i))
    stat_spec = pl.BlockSpec((hb, 2, rows), lambda i: (i, 0, 0))
    anywhere = pl.BlockSpec(memory_space=pl.ANY)
    cost = pl.CostEstimate(
        flops=24 * (reach + 1) * rows * rows * gw,
        bytes_accessed=(16 + 4 * reach) * rows * gw,
        transcendentals=0,
    )
    held, stats = (), []
    for g in range(groups):
        own = pl.BlockSpec((rows, bw), lambda i, g=g: (0, g * steps + i))
        fixed = 6 + reach
        *held, stat = pl.pallas_call(
            functools.partial(query_kernel, hb, width, reach, g == 0),
            grid=(steps,),
            in_specs=[col_spec, row_spec] + [own] * 4 + [far_spec] * reach + [anywhere] * len(held),
            out_specs=[own, own, stat_spec],
            out_shape=[full, full, jax.ShapeDtypeStruct((per_group, 2, rows), F32)],
            scratch_shapes=[bias],
            input_output_aliases={} if g == 0 else {fixed: 0, fixed + 1: 1},
            compiler_params=params,
            cost_estimate=cost,
            name="soft_queries",
        )(ids_col, row_before, soft_q, soft_grad_out, soft_k, soft_v, *before[g], *held)
        stats.append([stat] + relay(stat, "seq", -1, reach))
    soft_out, soft_dq = held
    held = ()
    for g in range(groups):
        own = pl.BlockSpec((rows, bw), lambda i, g=g: (0, g * steps + i))
        fixed = 7 + 2 * reach
        held = pl.pallas_call(
            functools.partial(key_kernel, hb, width, reach, g == 0),
            grid=(steps,),
            in_specs=[col_spec, row_spec]
            + [own] * 4
            + [stat_spec]
            + [far_spec] * reach
            + [stat_spec] * reach
            + [anywhere] * len(held),
            out_specs=[own, own],
            out_shape=[full, full],
            scratch_shapes=[bias],
            input_output_aliases={} if g == 0 else {fixed: 0, fixed + 1: 1},
            compiler_params=params,
            cost_estimate=cost,
            name="soft_keys",
        )(
            ids_col,
            row_after,
            soft_k,
            soft_v,
            soft_q,
            soft_grad_out,
            stats[g][0],
            *after[g],
            *stats[g][1:],
            *held,
        )
    soft_dk, soft_dv = held
    return (*light, soft_out, soft_dq, soft_dk, soft_dv)


def solution(mesh):
    wide = P(("dp", "seq"), "head")
    return jax.shard_map(
        per_device,
        mesh=mesh,
        in_specs=(P(("dp", "seq")), wide, wide, wide, P("head"), wide, wide, wide, wide, wide),
        out_specs=(wide,) * 8,
        check_vma=False,
    )
```

time: 653 us -> 182 us (0.28)
  the two profiles are of different devices: /device:TPU:28 before, /device:TPU:24 now
where the time goes in v1:
time: 182 us; the launch traced here: 181 us
  starting transfers between devices  82 us (45%)
  Pallas kernels  58.4 us (32%)
  waiting for transfers between devices  22.9 us (13%)
  local copies, waits for them, and re-layouts  8.3 us (5%)
  between operations  6.54 us (4%)
  other arithmetic  2.84 us (2%)
    ppermute x32, starting transfers between devices, shift(): lax.ppermute(value, axis, [(source, source + steps) for source in range(f...  82 us
    pallas_call x4, Pallas kernels, per_device(): pl.pallas_call(functools.partial(query_kernel, hb, width, reach, g == 0),...  23.3 us
    ppermute x32, waiting for transfers between devices, shift(): lax.ppermute(value, axis, [(source, source + steps) for source in range(f...  22.9 us
    pallas_call x4, Pallas kernels, per_device(): pl.pallas_call(functools.partial(key_kernel, hb, width, reach, g == 0), g...  18.2 us
    pallas_call x1, Pallas kernels, per_device(): pl.pallas_call(functools.partial(light_kernel, lhb, width, reach), grid=(...  10.4 us
    pallas_call x1, Pallas kernels, per_device(): pl.pallas_call(functools.partial(state_kernel, lhb, width), grid=(heads /...  6.46 us
  transfers between devices with their start and end apart: 32, of which 6 were waited for; matrix products, arithmetic and copies ran while one was open for 5% of the time, Pallas kernels for 30%

profile of v1, /device:TPU:24, one launch (start us, length us, event | category | flops | bytes accessed | tf_op | source)
XLA Modules:
  0.0 180.9 jit_solution(11221968129997151661)
XLA Ops:
  2.6 4.5 %collective-permute-start.2 = (s32[256]{0:T(256)S(1)}, s32[256]{0:T(256)S(1)}, u32[]{:S(2)}, u32[]{:S(2)}) collective-permute-start(s32[256]{0:T(256)S(1)} %broadcast_add_fusion), channel_id=1, source_target_pairs={{2,0},{4,2},{6,4},{3,1},{5,3},{7,5},{10,8},{12,10},{14,12},{11,9},... | collective-permute-start | bytes 3080 | tf_op jit(solution)/shard_map/ppermute | solution.py:24
  14.0 5.3 %collective-permute-start.28 = (bf16[2,256,512]{2,1,0:T(8,128)(2,1)}, bf16[2,256,512]{2,1,0:T(8,128)(2,1)}, u32[]{:S(2)}, u32[]{:S(2)}) collective-permute-start(bf16[2,256,512]{2,1,0:T(8,128)(2,1)} %pad_maximum_fusion.7), channel_id=1, source_target_pairs={{2,0},{4,2},{6,4},{3,1},{5,3},{7,5},{10,8},{12,10},{14,12},{11,9},... | collective-permute-start | bytes 1572872 | tf_op jit(solution)/shard_map/ppermute | solution.py:24
  20.0 6.5 %light_states.1 = (bf16[16,128,128]{2,1,0:T(8,128)(2,1)S(1)}, bf16[16,128,128]{2,1,0:T(8,128)(2,1)S(1)}) custom-call(f32[16]{0:T(128)S(1)} %copy-done.7, s32[256,1]{1,0:T(8,128)S(1)} %copy.31.ids_col, bf16[256,2048]{1,0:T(8,128)(2,1)S(1)} %copy-done, bf16[256,2048]{1,0:T(8,128)(2,1)S(1)} %copy-done.1, bf16[256,2048]{1,0:T(8,128)(2,1)} %v.7, bf16[256,2048]{1,0:T(8,128)(2,1)} %g.7), custom_call_target="tpu_custom_call" | custom-call | flops 268435456 | bytes 5242880 | tf_op jit(solution)/shard_map/light_states/pallas_call | solution.py:227
  28.9 4.7 %collective-permute-start.6 = (bf16[16,128,128]{2,1,0:T(8,128)(2,1)S(1)}, bf16[16,128,128]{2,1,0:T(8,128)(2,1)S(1)}, u32[]{:S(2)}, u32[]{:S(2)}) collective-permute-start(bf16[16,128,128]{2,1,0:T(8,128)(2,1)S(1)} %get-tuple-element.35), channel_id=1, source_target_pairs={{2,0},{4,2},{6,4},{3,1},{5,3},{7,5},{10,8},{12,10},{14,12},{11,9},... | collective-permute-start | bytes 1572872 | tf_op jit(solution)/shard_map/ppermute | solution.py:24
  35.3 5.7 %collective-permute-done.1 = s32[256]{0:T(256)S(1)} collective-permute-done((s32[256]{0:T(256)S(1)}, s32[256]{0:T(256)S(1)}, u32[]{:S(2)}, u32[]{:S(2)}) %collective-permute-start.1) | collective-permute-done | bytes 1056 | tf_op jit(solution)/shard_map/ppermute | solution.py:24
  45.1 4.8 %collective-permute-start.24 = (bf16[2,256,512]{2,1,0:T(8,128)(2,1)S(1)}, bf16[2,256,512]{2,1,0:T(8,128)(2,1)S(1)}, u32[]{:S(2)}, u32[]{:S(2)}) collective-permute-start(bf16[2,256,512]{2,1,0:T(8,128)(2,1)S(1)} %pad_maximum_fusion.6), channel_id=1, source_target_pairs={{2,0},{4,2},{6,4},{3,1},{5,3},{7,5},{10,8},{12,10},{14,12},{11,9},... | collective-permute-start | bytes 1572872 | tf_op jit(solution)/shard_map/ppermute | solution.py:24
  53.3 5.2 %collective-permute-start.7 = (bf16[16,128,128]{2,1,0:T(8,128)(2,1)S(1)}, bf16[16,128,128]{2,1,0:T(8,128)(2,1)S(1)}, u32[]{:S(2)}, u32[]{:S(2)}) collective-permute-start(bf16[16,128,128]{2,1,0:T(8,128)(2,1)S(1)} %collective-permute-done.6.rest_2_), channel_id=1, source_target_pairs={{2,0},{4,2},{6,4},{3,1},{5,3},{7,5},{10,8},{12,10},{14,12},{11,9},... | collective-permute-start | bytes 1572872 | tf_op jit(solution)/shard_map/ppermute | solution.py:24
  68.7 3.4 %collective-permute-done.10.rest_0_ = bf16[2,256,512]{2,1,0:T(8,128)(2,1)S(1)} collective-permute-done((bf16[2,256,512]{2,1,0:T(8,128)(2,1)S(1)}, bf16[2,256,512]{2,1,0:T(8,128)(2,1)S(1)}, u32[]{:S(2)}, u32[]{:S(2)}) %collective-permute-start.10) | collective-permute-done | bytes 524320 | tf_op jit(solution)/shard_map/ppermute | solution.py:24
  72.1 3.9 %collective-permute-start.20 = (bf16[2,256,512]{2,1,0:T(8,128)(2,1)S(1)}, bf16[2,256,512]{2,1,0:T(8,128)(2,1)S(1)}, u32[]{:S(2)}, u32[]{:S(2)}) collective-permute-start(bf16[2,256,512]{2,1,0:T(8,128)(2,1)S(1)} %pad_maximum_fusion.5), channel_id=1, source_target_pairs={{2,0},{4,2},{6,4},{3,1},{5,3},{7,5},{10,8},{12,10},{14,12},{11,9},... | collective-permute-start | bytes 1572872 | tf_op jit(solution)/shard_map/ppermute | solution.py:24
  76.0 7.3 %collective-permute-done.5.rest_1_ = bf16[16,128,128]{2,1,0:T(8,128)(2,1)S(1)} collective-permute-done((bf16[16,128,128]{2,1,0:T(8,128)(2,1)S(1)}, bf16[16,128,128]{2,1,0:T(8,128)(2,1)S(1)}, u32[]{:S(2)}, u32[]{:S(2)}) %collective-permute-start.5) | collective-permute-done | bytes 524320 | tf_op jit(solution)/shard_map/ppermute | solution.py:24
  85.9 10.4 %light.1 = (bf16[256,2048]{1,0:T(8,128)(2,1)}, bf16[256,2048]{1,0:T(8,128)(2,1)}, bf16[256,2048]{1,0:T(8,128)(2,1)}, bf16[256,2048]{1,0:T(8,128)(2,1)}) custom-call(f32[16]{0:T(128)S(1)} %copy-done.7, f32[2,16]{1,0:T(2,128)S(1)} %get-tuple-element.79.coef_f, f32[2,16]{1,0:T(2,128)S(1)} %get-tuple-element.78.coef_b, s32[256,1]{1,0:T(8,128)S(1)} %copy.31.ids_col, ...), custom_call_target="tpu_custom_call" | custom-call | flops 3221225472 | bytes 8388608 | tf_op jit(solution)/shard_map/light/pallas_call | solution.py:247
  96.3 5.2 %collective-permute-start.16 = (bf16[2,256,512]{2,1,0:T(8,128)(2,1)S(1)}, bf16[2,256,512]{2,1,0:T(8,128)(2,1)S(1)}, u32[]{:S(2)}, u32[]{:S(2)}) collective-permute-start(bf16[2,256,512]{2,1,0:T(8,128)(2,1)S(1)} %pad_maximum_fusion.4), channel_id=1, source_target_pairs={{2,0},{4,2},{6,4},{3,1},{5,3},{7,5},{10,8},{12,10},{14,12},{11,9},... | collective-permute-start | bytes 1572872 | tf_op jit(solution)/shard_map/ppermute | solution.py:24
  101.6 4.2 %collective-permute-done.15.rest_1_ = bf16[2,256,512]{2,1,0:T(8,128)(2,1)S(1)} collective-permute-done((bf16[2,256,512]{2,1,0:T(8,128)(2,1)}, bf16[2,256,512]{2,1,0:T(8,128)(2,1)S(1)}, u32[]{:S(2)}, u32[]{:S(2)}) %collective-permute-start.15) | collective-permute-done | bytes 524320 | tf_op jit(solution)/shard_map/ppermute | solution.py:24
  107.1 5.9 %soft_queries.4 = (bf16[256,2048]{1,0:T(8,128)(2,1)}, bf16[256,2048]{1,0:T(8,128)(2,1)}, f32[4,2,256]{2,1,0:T(2,128)S(1)}) custom-call(s32[256,1]{1,0:T(8,128)S(1)} %copy.31.ids_col, s32[1,768]{1,0:T(1,128)S(1)} %broadcast_in_dim.39.ids_row, bf16[256,2048]{1,0:T(8,128)(2,1)S(1)} %copy-done.2, bf16[256,2048]{1,0:T(8,128)(2,1)S(1)} %copy-done.4, ...), custom_call_target="tpu_custom_call" | custom-call | flops 2415919104 | bytes 3145728 | tf_op jit(solution)/shard_map/soft_queries/pallas_call | solution.py:289
  113.0 4.6 %collective-permute-start.29 = (bf16[2,256,512]{2,1,0:T(8,128)(2,1)}, bf16[2,256,512]{2,1,0:T(8,128)(2,1)S(1)}, u32[]{:S(2)}, u32[]{:S(2)}) collective-permute-start(bf16[2,256,512]{2,1,0:T(8,128)(2,1)} %collective-permute-done.28.rest_0_), channel_id=1, source_target_pairs={{2,0},{4,2},{6,4},{3,1},{5,3},{7,5},{10,8},{12,10},{14,12},{11,9},... | collective-permute-start | bytes 1572872 | tf_op jit(solution)/shard_map/ppermute | solution.py:24
  117.6 3.9 %collective-permute-start.25 = (bf16[2,256,512]{2,1,0:T(8,128)(2,1)S(1)}, bf16[2,256,512]{2,1,0:T(8,128)(2,1)S(1)}, u32[]{:S(2)}, u32[]{:S(2)}) collective-permute-start(bf16[2,256,512]{2,1,0:T(8,128)(2,1)S(1)} %collective-permute-done.24.rest_0_), channel_id=1, source_target_pairs={{2,0},{4,2},{6,4},{3,1},{5,3},{7,5},{10,8},{12,10},{14,12},{11,9},... | collective-permute-start | bytes 1572872 | tf_op jit(solution)/shard_map/ppermute | solution.py:24
  121.5 5.8 %soft_queries.5 = (bf16[256,2048]{1,0:T(8,128)(2,1)}, bf16[256,2048]{1,0:T(8,128)(2,1)}, f32[4,2,256]{2,1,0:T(2,128)S(1)}) custom-call(s32[256,1]{1,0:T(8,128)S(1)} %copy.31.ids_col, s32[1,768]{1,0:T(1,128)S(1)} %broadcast_in_dim.39.ids_row, bf16[256,2048]{1,0:T(8,128)(2,1)S(1)} %copy-done.2, ...), custom_call_target="tpu_custom_call", output_to_operand_aliasing={{0}: (8, {}), {1}: (9, {})} | custom-call | flops 2415919104 | bytes 3145728 | tf_op jit(solution)/shard_map/soft_queries/pallas_call | solution.py:289
  128.3 3.9 %collective-permute-start.30 = (f32[4,2,256]{2,1,0:T(2,128)S(1)}, f32[4,2,256]{2,1,0:T(2,128)S(1)}, u32[]{:S(2)}, u32[]{:S(2)}) collective-permute-start(f32[4,2,256]{2,1,0:T(2,128)S(1)} %get-tuple-element.51.stat0), channel_id=1, source_target_pairs={{2,0},{4,2},{6,4},{3,1},{5,3},{7,5},{10,8},{12,10},{14,12},{11,9},... | collective-permute-start | bytes 24584 | tf_op jit(solution)/shard_map/ppermute | solution.py:24
  132.2 5.8 %soft_queries.6 = (bf16[256,2048]{1,0:T(8,128)(2,1)}, bf16[256,2048]{1,0:T(8,128)(2,1)}, f32[4,2,256]{2,1,0:T(2,128)S(1)}) custom-call(s32[256,1]{1,0:T(8,128)S(1)} %copy.31.ids_col, s32[1,768]{1,0:T(1,128)S(1)} %broadcast_in_dim.39.ids_row, bf16[256,2048]{1,0:T(8,128)(2,1)S(1)} %copy-done.2, ...), custom_call_target="tpu_custom_call", output_to_operand_aliasing={{0}: (8, {}), {1}: (9, {})} | custom-call | flops 2415919104 | bytes 3145728 | tf_op jit(solution)/shard_map/soft_queries/pallas_call | solution.py:289
  145.1 5.9 %soft_queries.7 = (bf16[256,2048]{1,0:T(8,128)(2,1)}, bf16[256,2048]{1,0:T(8,128)(2,1)}, f32[4,2,256]{2,1,0:T(2,128)S(1)}) custom-call(s32[256,1]{1,0:T(8,128)S(1)} %copy.31.ids_col, s32[1,768]{1,0:T(1,128)S(1)} %broadcast_in_dim.39.ids_row, bf16[256,2048]{1,0:T(8,128)(2,1)S(1)} %copy-done.2, ...), custom_call_target="tpu_custom_call", output_to_operand_aliasing={{0}: (8, {}), {1}: (9, {})} | custom-call | flops 2415919104 | bytes 3145728 | tf_op jit(solution)/shard_map/soft_queries/pallas_call | solution.py:289
  158.8 4.6 %soft_keys.4 = (bf16[256,2048]{1,0:T(8,128)(2,1)}, bf16[256,2048]{1,0:T(8,128)(2,1)}) custom-call(s32[256,1]{1,0:T(8,128)S(1)} %copy.31.ids_col, s32[1,768]{1,0:T(1,128)S(1)} %broadcast_in_dim.40.ids_row, bf16[256,2048]{1,0:T(8,128)(2,1)S(1)} %copy-done.5, bf16[256,2048]{1,0:T(8,128)(2,1)S(1)} %copy-done.6, bf16[256,2048]{1,0:T(8,128)(2,1)} %q0.7, ...), custom_call_target="tpu_custom_call" | custom-call | flops 2415919104 | bytes 3145728 | tf_op jit(solution)/shard_map/soft_keys/pallas_call | solution.py:307
  167.3 4.5 %soft_keys.5 = (bf16[256,2048]{1,0:T(8,128)(2,1)}, bf16[256,2048]{1,0:T(8,128)(2,1)}) custom-call(s32[256,1]{1,0:T(8,128)S(1)} %copy.31.ids_col, s32[1,768]{1,0:T(1,128)S(1)} %broadcast_in_dim.40.ids_row, bf16[256,2048]{1,0:T(8,128)(2,1)S(1)} %copy-done.5, bf16[256,2048]{1,0:T(8,128)(2,1)S(1)} %copy-done.6, ...), custom_call_target="tpu_custom_call", output_to_operand_aliasing={{0}: (11, {}), {1}: (12, {})} | custom-call | flops 2415919104 | bytes 3145728 | tf_op jit(solution)/shard_map/soft_keys/pallas_call | solution.py:307
  171.9 4.5 %soft_keys.6 = (bf16[256,2048]{1,0:T(8,128)(2,1)}, bf16[256,2048]{1,0:T(8,128)(2,1)}) custom-call(s32[256,1]{1,0:T(8,128)S(1)} %copy.31.ids_col, s32[1,768]{1,0:T(1,128)S(1)} %broadcast_in_dim.40.ids_row, bf16[256,2048]{1,0:T(8,128)(2,1)S(1)} %copy-done.5, bf16[256,2048]{1,0:T(8,128)(2,1)S(1)} %copy-done.6, ...), custom_call_target="tpu_custom_call", output_to_operand_aliasing={{0}: (11, {}), {1}: (12, {})} | custom-call | flops 2415919104 | bytes 3145728 | tf_op jit(solution)/shard_map/soft_keys/pallas_call | solution.py:307
  176.4 4.5 %soft_keys.7 = (bf16[256,2048]{1,0:T(8,128)(2,1)}, bf16[256,2048]{1,0:T(8,128)(2,1)}) custom-call(s32[256,1]{1,0:T(8,128)S(1)} %copy.31.ids_col, s32[1,768]{1,0:T(1,128)S(1)} %broadcast_in_dim.40.ids_row, bf16[256,2048]{1,0:T(8,128)(2,1)S(1)} %copy-done.5, bf16[256,2048]{1,0:T(8,128)(2,1)S(1)} %copy-done.6, ...), custom_call_target="tpu_custom_call", output_to_operand_aliasing={{0}: (11, {}), {1}: (12, {})} | custom-call | flops 2415919104 | bytes 3145728 | tf_op jit(solution)/shard_map/soft_keys/pallas_call | solution.py:307
  (112 shorter events, 49.2 us)
Async XLA Ops:
  1.3 27.6 %collective-permute-start = (s32[256]{0:T(256)S(1)}, s32[256]{0:T(256)S(1)}, u32[]{:S(2)}, u32[]{:S(2)}) collective-permute-start(s32[256]{0:T(256)S(1)} %broadcast_add_fusion), channel_id=1, source_target_pairs={{0,2},{2,4},{4,6},{1,3},{3,5},{5,7},{8,10},{10,12},{12,14},{9,11},... | collective-permute-start | bytes 3080 | tf_op jit(solution)/shard_map/ppermute | solution.py:24
  2.6 31.1 %collective-permute-start.2 = (s32[256]{0:T(256)S(1)}, s32[256]{0:T(256)S(1)}, u32[]{:S(2)}, u32[]{:S(2)}) collective-permute-start(s32[256]{0:T(256)S(1)} %broadcast_add_fusion), channel_id=1, source_target_pairs={{2,0},{4,2},{6,4},{3,1},{5,3},{7,5},{10,8},{12,10},{14,12},{11,9},... | collective-permute-start | bytes 3080 | tf_op jit(solution)/shard_map/ppermute | solution.py:24
  10.8 34.4 %collective-permute-start.14 = (bf16[2,256,512]{2,1,0:T(8,128)(2,1)}, bf16[2,256,512]{2,1,0:T(8,128)(2,1)}, u32[]{:S(2)}, u32[]{:S(2)}) collective-permute-start(bf16[2,256,512]{2,1,0:T(8,128)(2,1)} %pad_maximum_fusion.3), channel_id=1, source_target_pairs={{0,2},{2,4},{4,6},{1,3},{3,5},{5,7},{8,10},{10,12},{12,14},{9,11},... | collective-permute-start | bytes 1572872 | tf_op jit(solution)/shard_map/ppermute | solution.py:24
  14.0 36.6 %collective-permute-start.28 = (bf16[2,256,512]{2,1,0:T(8,128)(2,1)}, bf16[2,256,512]{2,1,0:T(8,128)(2,1)}, u32[]{:S(2)}, u32[]{:S(2)}) collective-permute-start(bf16[2,256,512]{2,1,0:T(8,128)(2,1)} %pad_maximum_fusion.7), channel_id=1, source_target_pairs={{2,0},{4,2},{6,4},{3,1},{5,3},{7,5},{10,8},{12,10},{14,12},{11,9},... | collective-permute-start | bytes 1572872 | tf_op jit(solution)/shard_map/ppermute | solution.py:24
  26.5 25.4 %collective-permute-start.4 = (bf16[16,128,128]{2,1,0:T(8,128)(2,1)S(1)}, bf16[16,128,128]{2,1,0:T(8,128)(2,1)S(1)}, u32[]{:S(2)}, u32[]{:S(2)}) collective-permute-start(bf16[16,128,128]{2,1,0:T(8,128)(2,1)S(1)} %get-tuple-element.34), channel_id=1, source_target_pairs={{0,2},{2,4},{4,6},{1,3},{3,5},{5,7},{8,10},{10,12},{12,14},{9,11},... | collective-permute-start | bytes 1572872 | tf_op jit(solution)/shard_map/ppermute | solution.py:24
  28.9 24.3 %collective-permute-start.6 = (bf16[16,128,128]{2,1,0:T(8,128)(2,1)S(1)}, bf16[16,128,128]{2,1,0:T(8,128)(2,1)S(1)}, u32[]{:S(2)}, u32[]{:S(2)}) collective-permute-start(bf16[16,128,128]{2,1,0:T(8,128)(2,1)S(1)} %get-tuple-element.35), channel_id=1, source_target_pairs={{2,0},{4,2},{6,4},{3,1},{5,3},{7,5},{10,8},{12,10},{14,12},{11,9},... | collective-permute-start | bytes 1572872 | tf_op jit(solution)/shard_map/ppermute | solution.py:24
  43.8 22.2 %collective-permute-start.12 = (bf16[2,256,512]{2,1,0:T(8,128)(2,1)S(1)}, bf16[2,256,512]{2,1,0:T(8,128)(2,1)S(1)}, u32[]{:S(2)}, u32[]{:S(2)}) collective-permute-start(bf16[2,256,512]{2,1,0:T(8,128)(2,1)S(1)} %pad_maximum_fusion.2), channel_id=1, source_target_pairs={{0,2},{2,4},{4,6},{1,3},{3,5},{5,7},{8,10},{10,12},{12,14},{9,11},... | collective-permute-start | bytes 1572872 | tf_op jit(solution)/shard_map/ppermute | solution.py:24
  45.1 22.2 %collective-permute-start.24 = (bf16[2,256,512]{2,1,0:T(8,128)(2,1)S(1)}, bf16[2,256,512]{2,1,0:T(8,128)(2,1)S(1)}, u32[]{:S(2)}, u32[]{:S(2)}) collective-permute-start(bf16[2,256,512]{2,1,0:T(8,128)(2,1)S(1)} %pad_maximum_fusion.6), channel_id=1, source_target_pairs={{2,0},{4,2},{6,4},{3,1},{5,3},{7,5},{10,8},{12,10},{14,12},{11,9},... | collective-permute-start | bytes 1572872 | tf_op jit(solution)/shard_map/ppermute | solution.py:24
  50.6 21.4 %collective-permute-start.10 = (bf16[2,256,512]{2,1,0:T(8,128)(2,1)S(1)}, bf16[2,256,512]{2,1,0:T(8,128)(2,1)S(1)}, u32[]{:S(2)}, u32[]{:S(2)}) collective-permute-start(bf16[2,256,512]{2,1,0:T(8,128)(2,1)S(1)} %pad_maximum_fusion.1), channel_id=1, source_target_pairs={{0,2},{2,4},{4,6},{1,3},{3,5},{5,7},{8,10},{10,12},{12,14},{9,11},... | collective-permute-start | bytes 1572872 | tf_op jit(solution)/shard_map/ppermute | solution.py:24
  51.9 31.4 %collective-permute-start.5 = (bf16[16,128,128]{2,1,0:T(8,128)(2,1)S(1)}, bf16[16,128,128]{2,1,0:T(8,128)(2,1)S(1)}, u32[]{:S(2)}, u32[]{:S(2)}) collective-permute-start(bf16[16,128,128]{2,1,0:T(8,128)(2,1)S(1)} %collective-permute-done.4.rest_0_), channel_id=1, source_target_pairs={{0,2},{2,4},{4,6},{1,3},{3,5},{5,7},{8,10},{10,12},{12,14},{9,11},... | collective-permute-start | bytes 1572872 | tf_op jit(solution)/shard_map/ppermute | solution.py:24
  53.3 31.3 %collective-permute-start.7 = (bf16[16,128,128]{2,1,0:T(8,128)(2,1)S(1)}, bf16[16,128,128]{2,1,0:T(8,128)(2,1)S(1)}, u32[]{:S(2)}, u32[]{:S(2)}) collective-permute-start(bf16[16,128,128]{2,1,0:T(8,128)(2,1)S(1)} %collective-permute-done.6.rest_2_), channel_id=1, source_target_pairs={{2,0},{4,2},{6,4},{3,1},{5,3},{7,5},{10,8},{12,10},{14,12},{11,9},... | collective-permute-start | bytes 1572872 | tf_op jit(solution)/shard_map/ppermute | solution.py:24
  66.0 30.3 %collective-permute-start.8 = (bf16[2,256,512]{2,1,0:T(8,128)(2,1)S(1)}, bf16[2,256,512]{2,1,0:T(8,128)(2,1)S(1)}, u32[]{:S(2)}, u32[]{:S(2)}) collective-permute-start(bf16[2,256,512]{2,1,0:T(8,128)(2,1)S(1)} %pad_maximum_fusion), channel_id=1, source_target_pairs={{0,2},{2,4},{4,6},{1,3},{3,5},{5,7},{8,10},{10,12},{12,14},{9,11},... | collective-permute-start | bytes 1572872 | tf_op jit(solution)/shard_map/ppermute | solution.py:24
  67.3 38.5 %collective-permute-start.15 = (bf16[2,256,512]{2,1,0:T(8,128)(2,1)}, bf16[2,256,512]{2,1,0:T(8,128)(2,1)S(1)}, u32[]{:S(2)}, u32[]{:S(2)}) collective-permute-start(bf16[2,256,512]{2,1,0:T(8,128)(2,1)} %collective-permute-done.14.rest_0_), channel_id=1, source_target_pairs={{0,2},{2,4},{4,6},{1,3},{3,5},{5,7},{8,10},{10,12},{12,14},{9,11},... | collective-permute-start | bytes 1572872 | tf_op jit(solution)/shard_map/ppermute | solution.py:24
  72.1 40.9 %collective-permute-start.20 = (bf16[2,256,512]{2,1,0:T(8,128)(2,1)S(1)}, bf16[2,256,512]{2,1,0:T(8,128)(2,1)S(1)}, u32[]{:S(2)}, u32[]{:S(2)}) collective-permute-start(bf16[2,256,512]{2,1,0:T(8,128)(2,1)S(1)} %pad_maximum_fusion.5), channel_id=1, source_target_pairs={{2,0},{4,2},{6,4},{3,1},{5,3},{7,5},{10,8},{12,10},{14,12},{11,9},... | collective-permute-start | bytes 1572872 | tf_op jit(solution)/shard_map/ppermute | solution.py:24
  83.3 34.2 %collective-permute-start.13 = (bf16[2,256,512]{2,1,0:T(8,128)(2,1)S(1)}, bf16[2,256,512]{2,1,0:T(8,128)(2,1)S(1)}, u32[]{:S(2)}, u32[]{:S(2)}) collective-permute-start(bf16[2,256,512]{2,1,0:T(8,128)(2,1)S(1)} %collective-permute-done.12.rest_0_), channel_id=1, source_target_pairs={{0,2},{2,4},{4,6},{1,3},{3,5},{5,7},{8,10},{10,12},{12,14},{9,11},... | collective-permute-start | bytes 1572872 | tf_op jit(solution)/shard_map/ppermute | solution.py:24
  84.6 43.6 %collective-permute-start.11 = (bf16[2,256,512]{2,1,0:T(8,128)(2,1)S(1)}, bf16[2,256,512]{2,1,0:T(8,128)(2,1)S(1)}, u32[]{:S(2)}, u32[]{:S(2)}) collective-permute-start(bf16[2,256,512]{2,1,0:T(8,128)(2,1)S(1)} %collective-permute-done.10.rest_0_), channel_id=1, source_target_pairs={{0,2},{2,4},{4,6},{1,3},{3,5},{5,7},{8,10},{10,12},{12,14},{9,11},... | collective-permute-start | bytes 1572872 | tf_op jit(solution)/shard_map/ppermute | solution.py:24
  96.3 41.6 %collective-permute-start.16 = (bf16[2,256,512]{2,1,0:T(8,128)(2,1)S(1)}, bf16[2,256,512]{2,1,0:T(8,128)(2,1)S(1)}, u32[]{:S(2)}, u32[]{:S(2)}) collective-permute-start(bf16[2,256,512]{2,1,0:T(8,128)(2,1)S(1)} %pad_maximum_fusion.4), channel_id=1, source_target_pairs={{2,0},{4,2},{6,4},{3,1},{5,3},{7,5},{10,8},{12,10},{14,12},{11,9},... | collective-permute-start | bytes 1572872 | tf_op jit(solution)/shard_map/ppermute | solution.py:24
  105.8 35.3 %collective-permute-start.9 = (bf16[2,256,512]{2,1,0:T(8,128)(2,1)S(1)}, bf16[2,256,512]{2,1,0:T(8,128)(2,1)S(1)}, u32[]{:S(2)}, u32[]{:S(2)}) collective-permute-start(bf16[2,256,512]{2,1,0:T(8,128)(2,1)S(1)} %collective-permute-done.8.rest_0_), channel_id=1, source_target_pairs={{0,2},{2,4},{4,6},{1,3},{3,5},{5,7},{8,10},{10,12},{12,14},{9,11},... | collective-permute-start | bytes 1572872 | tf_op jit(solution)/shard_map/ppermute | solution.py:24
  113.0 38.1 %collective-permute-start.29 = (bf16[2,256,512]{2,1,0:T(8,128)(2,1)}, bf16[2,256,512]{2,1,0:T(8,128)(2,1)S(1)}, u32[]{:S(2)}, u32[]{:S(2)}) collective-permute-start(bf16[2,256,512]{2,1,0:T(8,128)(2,1)} %collective-permute-done.28.rest_0_), channel_id=1, source_target_pairs={{2,0},{4,2},{6,4},{3,1},{5,3},{7,5},{10,8},{12,10},{14,12},{11,9},... | collective-permute-start | bytes 1572872 | tf_op jit(solution)/shard_map/ppermute | solution.py:24
  117.6 35.4 %collective-permute-start.25 = (bf16[2,256,512]{2,1,0:T(8,128)(2,1)S(1)}, bf16[2,256,512]{2,1,0:T(8,128)(2,1)S(1)}, u32[]{:S(2)}, u32[]{:S(2)}) collective-permute-start(bf16[2,256,512]{2,1,0:T(8,128)(2,1)S(1)} %collective-permute-done.24.rest_0_), channel_id=1, source_target_pairs={{2,0},{4,2},{6,4},{3,1},{5,3},{7,5},{10,8},{12,10},{14,12},{11,9},... | collective-permute-start | bytes 1572872 | tf_op jit(solution)/shard_map/ppermute | solution.py:24
  128.3 14.7 %collective-permute-start.30 = (f32[4,2,256]{2,1,0:T(2,128)S(1)}, f32[4,2,256]{2,1,0:T(2,128)S(1)}, u32[]{:S(2)}, u32[]{:S(2)}) collective-permute-start(f32[4,2,256]{2,1,0:T(2,128)S(1)} %get-tuple-element.51.stat0), channel_id=1, source_target_pairs={{2,0},{4,2},{6,4},{3,1},{5,3},{7,5},{10,8},{12,10},{14,12},{11,9},... | collective-permute-start | bytes 24584 | tf_op jit(solution)/shard_map/ppermute | solution.py:24
  138.0 33.9 %collective-permute-start.21 = (bf16[2,256,512]{2,1,0:T(8,128)(2,1)S(1)}, bf16[2,256,512]{2,1,0:T(8,128)(2,1)S(1)}, u32[]{:S(2)}, u32[]{:S(2)}) collective-permute-start(bf16[2,256,512]{2,1,0:T(8,128)(2,1)S(1)} %collective-permute-done.20.rest_0_), channel_id=1, source_target_pairs={{2,0},{4,2},{6,4},{3,1},{5,3},{7,5},{10,8},{12,10},{14,12},{11,9},... | collective-permute-start | bytes 1572872 | tf_op jit(solution)/shard_map/ppermute | solution.py:24
  143.0 13.8 %collective-permute-start.31 = (f32[4,2,256]{2,1,0:T(2,128)S(1)}, f32[4,2,256]{2,1,0:T(2,128)S(1)}, u32[]{:S(2)}, u32[]{:S(2)}) collective-permute-start(f32[4,2,256]{2,1,0:T(2,128)S(1)} %collective-permute-done.30.rest_2_), channel_id=1, source_target_pairs={{2,0},{4,2},{6,4},{3,1},{5,3},{7,5},{10,8},{12,10},{14,12},{11,9},... | collective-permute-start | bytes 24584 | tf_op jit(solution)/shard_map/ppermute | solution.py:24
  151.0 25.3 %collective-permute-start.17 = (bf16[2,256,512]{2,1,0:T(8,128)(2,1)S(1)}, bf16[2,256,512]{2,1,0:T(8,128)(2,1)S(1)}, u32[]{:S(2)}, u32[]{:S(2)}) collective-permute-start(bf16[2,256,512]{2,1,0:T(8,128)(2,1)S(1)} %collective-permute-done.16.rest_0_), channel_id=1, source_target_pairs={{2,0},{4,2},{6,4},{3,1},{5,3},{7,5},{10,8},{12,10},{14,12},{11,9},... | collective-permute-start | bytes 1572872 | tf_op jit(solution)/shard_map/ppermute | solution.py:24
  (27 other events, 197.5 us)

commit v2 on v1

v2 whole, which is shorter than its diff:
```python
import functools
import math

import jax
import jax.numpy as jnp
from jax import lax
from jax.experimental import pallas as pl
from jax.experimental.pallas import tpu as pltpu
from jax.sharding import PartitionSpec as P

NEG = -1e30
F32 = jnp.float32
BF16 = jnp.bfloat16
VMEM_LIMIT = 50 * 1024 * 1024


def mm(a, b, ca, cb):
    return lax.dot_general(a, b, (((ca,), (cb,)), ((), ())), preferred_element_type=F32)


def attention_kernel(
    shards,
    reach,
    heads,
    hb,
    decay,
    ids_col,
    ids_row,
    lq,
    lk,
    lv,
    lg,
    sq,
    sk,
    sv,
    sg,
    l_out,
    l_dq,
    l_dk,
    l_dv,
    s_out,
    s_dq,
    s_dk,
    s_dv,
    slots,
    states,
    own_states,
    stats,
    own_stats,
    ids_slots,
    bias_q,
    bias_k,
    dist,
    send_sem,
    recv_sem,
    state_send,
    state_recv,
    stat_send,
    stat_recv,
    ids_send,
    ids_recv,
):
    rows, all_cols = lq.shape
    width = all_cols // heads
    chunks = heads // hb
    cw = hb * width
    me = lax.axis_index("seq")
    scale = width ** -0.5
    unit = scale * math.log2(math.e)
    wide_own = (sk, sv, sq, sg)
    way_of = (1, 1, -1, -1)

    def col(c, n=None):
        n = cw if n is None else n
        return pl.ds(pl.multiple_of(c * n, n), n)

    def sends(way, hop):
        if way > 0:
            return (me >= hop) & (me + 1 < shards)
        return (me + hop < shards) & (me >= 1)

    def takes(way, hop):
        return me >= hop + 1 if way > 0 else me + hop + 1 < shards

    def wide_copy(kind, hop, c):
        source = wide_own[kind].at[:, col(c)] if hop == 0 else slots.at[kind, hop - 1, :, col(c)]
        return pltpu.make_async_remote_copy(
            src_ref=source,
            dst_ref=slots.at[kind, hop, :, col(c)],
            send_sem=send_sem.at[kind, hop, c],
            recv_sem=recv_sem.at[kind, hop, c],
            device_id={"seq": me + way_of[kind]},
            device_id_type=pl.DeviceIdType.MESH,
        )

    def state_copy(kind, hop, c):
        part = pl.ds(c * hb, hb)
        source = own_states.at[kind, part] if hop == 0 else states.at[kind, hop - 1, part]
        return pltpu.make_async_remote_copy(
            src_ref=source,
            dst_ref=states.at[kind, hop, part],
            send_sem=state_send.at[kind, hop, c],
            recv_sem=state_recv.at[kind, hop, c],
            device_id={"seq": me + (1, -1)[kind]},
            device_id_type=pl.DeviceIdType.MESH,
        )

    def stat_copy(hop, c):
        part = pl.ds(c * hb, hb)
        source = own_stats.at[part] if hop == 0 else stats.at[hop - 1, part]
        return pltpu.make_async_remote_copy(
            src_ref=source,
            dst_ref=stats.at[hop, part],
            send_sem=stat_send.at[hop, c],
            recv_sem=stat_recv.at[hop, c],
            device_id={"seq": me - 1},
            device_id_type=pl.DeviceIdType.MESH,
        )

    def ids_copy(kind, hop):
        return pltpu.make_async_remote_copy(
            src_ref=ids_row if hop == 0 else ids_slots.at[kind, hop - 1],
            dst_ref=ids_slots.at[kind, hop],
            send_sem=ids_send.at[kind, hop],
            recv_sem=ids_recv.at[kind, hop],
            device_id={"seq": me + (1, -1)[kind]},
            device_id_type=pl.DeviceIdType.MESH,
        )

    def start_wide(hop, c):
        for way, kinds in ((1, (0, 1)), (-1, (2, 3))):

            @pl.when(sends(way, hop))
            def _():
                for kind in kinds:
                    wide_copy(kind, hop, c).start()

    def start_states(hop, c):
        for kind, way in enumerate((1, -1)):

            @pl.when(sends(way, hop))
            def _():
                state_copy(kind, hop, c).start()

    def await_chunk(hop, c):
        for way, kinds in ((1, (0, 1)), (-1, (2, 3))):

            @pl.when(takes(way, hop))
            def _():
                for kind in kinds:
                    wide_copy(kind, hop, c).wait_recv()
                state_copy(0 if way > 0 else 1, hop, c).wait_recv()

    ids = ids_col[...]
    pos = lax.broadcasted_iota(jnp.int32, (rows, width), 0).astype(F32)
    lane = lax.broadcasted_iota(jnp.int32, (rows, width), 1)
    head_on = jnp.where(ids == ids_col[0:1, :], 0.0, NEG)
    tail_on = jnp.where(ids == ids_col[rows - 1 : rows, :], 0.0, NEG)

    def make_states(c):
        for j in range(hb):
            h = c * hb + j
            lam = decay[h]
            cols = col(h, width)
            to_end = jnp.exp(tail_on - lam * (rows - 1.0 - pos))
            since = jnp.exp(head_on - lam * (pos + 1.0))
            kd = (lk[:, cols].astype(F32) * to_end).astype(BF16)
            qd = (lq[:, cols].astype(F32) * since).astype(BF16)
            own_states[0, h] = mm(kd, lv[:, cols], 0, 0).astype(BF16)
            own_states[1, h] = mm(qd, lg[:, cols], 0, 0).astype(BF16)

    def light(c):
        for j in range(hb):
            h = c * hb + j
            lam = decay[h]
            cols = col(h, width)
            qh, kh, vh, gh = lq[:, cols], lk[:, cols], lv[:, cols], lg[:, cols]
            state = later = None
            for d in range(reach):
                keep = jnp.exp(jnp.zeros((1, width), F32) - lam * (rows * d))
                met = ids_slots[0, d, :, rows - 1 : rows] == ids_col[0:1, :]
                left = ids_slots[1, d, :, 0:1] == ids_col[rows - 1 : rows, :]
                ahead = jnp.where(met, keep, 0.0) * states[0, d, h].astype(F32)
                back = jnp.where(left, keep, 0.0) * states[1, d, h].astype(F32)
                state = ahead if state is None else state + ahead
                later = back if later is None else later + back
            state, later = state.astype(BF16), later.astype(BF16)
            to_end = jnp.exp(tail_on - lam * (rows - 1.0 - pos))
            since = jnp.exp(head_on - lam * (pos + 1.0))
            weight = jnp.exp(bias_q[0] - lam * dist[...])
            scores = (mm(qh, kh, 1, 1) * weight).astype(BF16)
            grads = (mm(gh, vh, 1, 1) * weight).astype(BF16)
            l_out[:, cols] = (mm(scores, vh, 1, 0) + mm(qh, state, 1, 0) * since).astype(BF16)
            l_dq[:, cols] = (mm(grads, kh, 1, 0) + mm(gh, state, 1, 1) * since).astype(BF16)
            l_dk[:, cols] = (mm(grads, qh, 0, 0) + mm(vh, later, 1, 1) * to_end).astype(BF16)
            l_dv[:, cols] = (mm(scores, gh, 0, 0) + mm(kh, later, 1, 0) * to_end).astype(BF16)

    def queries(c):
        for j in range(hb):
            h = c * hb + j
            cols = col(h, width)
            qh, gh = sq[:, cols], sg[:, cols]
            keys = [sk[:, cols]] + [slots[0, d, :, cols] for d in range(reach)]
            values = [sv[:, cols]] + [slots[1, d, :, cols] for d in range(reach)]
            raw = [mm(qh, kh, 1, 1) + bias_q[d] for d, kh in enumerate(keys)]
            top = functools.reduce(jnp.maximum, raw).max(axis=1, keepdims=True)
            expo = [jnp.exp2((r - top) * unit) for r in raw]
            total = functools.reduce(jnp.add, expo).sum(axis=1, keepdims=True)
            acc = functools.reduce(
                jnp.add, [mm(e.astype(BF16), vh, 1, 0) for e, vh in zip(expo, values)]
            )
            inv = 1.0 / total
            o16 = (acc * inv).astype(BF16)
            s_out[:, cols] = o16
            delta = (gh.astype(F32) * o16.astype(F32)).sum(axis=1, keepdims=True)
            lse = top + jnp.log(total) * (1.0 / scale)
            acc = None
            for e, kh, vh in zip(expo, keys, values):
                ds = ((e * inv) * (mm(gh, vh, 1, 1) - delta)).astype(BF16)
                part = mm(ds, kh, 1, 0)
                acc = part if acc is None else acc + part
            s_dq[:, cols] = (acc * scale).astype(BF16)
            own_stats[h] = jnp.where(lane == 0, lse, delta).T[0:8, :]

    def keys_side(c):
        for j in range(hb):
            h = c * hb + j
            cols = col(h, width)
            kh, vh = sk[:, cols], sv[:, cols]
            dk_acc = dv_acc = None
            for d in range(reach + 1):
                qh = sq[:, cols] if d == 0 else slots[2, d - 1, :, cols]
                gh = sg[:, cols] if d == 0 else slots[3, d - 1, :, cols]
                st = own_stats[h] if d == 0 else stats[d - 1, h]
                lse, delta = st[0:1, :], st[1:2, :]
                raw = mm(kh, qh, 1, 1) + bias_k[d]
                prob = jnp.exp2((raw - lse) * unit)
                ds = (prob * (mm(vh, gh, 1, 1) - delta)).astype(BF16)
                dv_part = mm(prob.astype(BF16), gh, 1, 0)
                dk_part = mm(ds, qh, 1, 0)
                dk_acc = dk_part if dk_acc is None else dk_acc + dk_part
                dv_acc = dv_part if dv_acc is None else dv_acc + dv_part
            s_dk[:, cols] = (dk_acc * scale).astype(BF16)
            s_dv[:, cols] = dv_acc.astype(BF16)

    barrier = pltpu.get_barrier_semaphore()
    for way, there in ((-1, me >= 1), (1, me + 1 < shards)):

        @pl.when(there)
        def _():
            pl.semaphore_signal(
                barrier, 1, device_id={"seq": me + way}, device_id_type=pl.DeviceIdType.MESH
            )

    pl.semaphore_wait(barrier, jnp.where((me == 0) | (me == shards - 1), 1, 2))

    for kind, way in enumerate((1, -1)):

        @pl.when(sends(way, 0))
        def _():
            ids_copy(kind, 0).start()

    start_wide(0, 0)
    make_states(0)
    start_states(0, 0)

    for d in range(reach):
        for way, kinds in ((1, (0, 1)), (-1, (2, 3))):

            @pl.when(jnp.logical_not(takes(way, d)))
            def _():
                for kind in kinds:
                    slots[kind, d] = jnp.zeros((rows, all_cols), BF16)
                one = kinds[0] // 2
                states[one, d] = jnp.zeros((heads, width, width), BF16)
                ids_slots[one, d] = jnp.zeros((1, rows), jnp.int32)
                if way < 0:
                    stats[d] = jnp.zeros((heads, 8, rows), F32)

    t = lax.broadcasted_iota(jnp.int32, (rows, rows), 0)
    s = lax.broadcasted_iota(jnp.int32, (rows, rows), 1)
    same = ids == ids_row[...]
    bias_q[0] = jnp.where(same & (s <= t), 0.0, NEG)
    bias_k[0] = jnp.where(same & (t <= s), 0.0, NEG)
    dist[...] = jnp.maximum(t - s, 0).astype(F32)
    for d in range(reach):
        for kind, way in enumerate((1, -1)):

            @pl.when(takes(way, d))
            def _():
                ids_copy(kind, d).wait_recv()

            if d + 1 < reach:

                @pl.when(sends(way, d + 1))
                def _():
                    ids_copy(kind, d + 1).start()

    for d in range(reach):
        bias_q[d + 1] = jnp.where(ids == ids_slots[0, d], 0.0, NEG)
        bias_k[d + 1] = jnp.where(ids == ids_slots[1, d], 0.0, NEG)

    def step(at, carry):
        @pl.when(at + 1 < chunks)
        def _():
            start_wide(0, at + 1)
            make_states(at + 1)
            start_states(0, at + 1)

        for d in range(reach - 1):

            @pl.when((at >= d) & (at - d < chunks))
            def _():
                await_chunk(d, at - d)
                start_wide(d + 1, at - d)
                start_states(d + 1, at - d)

        mid = at - (reach - 1)

        @pl.when((mid >= 0) & (mid < chunks))
        def _():
            await_chunk(reach - 1, mid)
            queries(mid)

            @pl.when(sends(-1, 0))
            def _():
                stat_copy(0, mid).start()

            light(mid)

        for d in range(reach - 1):

            @pl.when((mid >= d) & (mid - d < chunks))
            def _():
                @pl.when(takes(-1, d))
                def _():
                    stat_copy(d, mid - d).wait_recv()

                @pl.when(sends(-1, d + 1))
                def _():
                    stat_copy(d + 1, mid - d).start()

        last = mid - (reach - 1)

        @pl.when((last >= 0) & (last < chunks))
        def _():
            @pl.when(takes(-1, reach - 1))
            def _():
                stat_copy(reach - 1, last).wait_recv()

            keys_side(last)

        return carry

    lax.fori_loop(0, chunks + 2 * (reach - 1), step, 0)

    for hop in range(reach):
        for way, kinds in ((1, (0, 1)), (-1, (2, 3))):

            @pl.when(sends(way, hop))
            def _():
                one = kinds[0] // 2
                ids_copy(one, hop).wait_send()

                def drain(c, carry):
                    for kind in kinds:
                        wide_copy(kind, hop, c).wait_send()
                    state_copy(one, hop, c).wait_send()
                    if way < 0:
                        stat_copy(hop, c).wait_send()
                    return carry

                lax.fori_loop(0, chunks, drain, 0)


def per_device(doc_ids, light_q, light_k, light_v, light_decay, light_grad_out, *soft):
    rows, cols = light_q.shape
    heads = light_decay.shape[0]
    width = cols // heads
    shards = lax.axis_size("seq")
    total_rows = rows * shards
    reach = min(shards - 1, (rows + total_rows // 2 - 2) // rows)
    hb = 2 if heads % 2 == 0 else 1
    chunks = heads // hb
    ids = doc_ids + 1
    vmem = pl.BlockSpec(memory_space=pltpu.VMEM)
    dma = pltpu.SemaphoreType.DMA
    return pl.pallas_call(
        functools.partial(attention_kernel, shards, reach, heads, hb),
        in_specs=[pl.BlockSpec(memory_space=pltpu.SMEM)] + [vmem] * 10,
        out_specs=[vmem] * 8,
        out_shape=[jax.ShapeDtypeStruct((rows, cols), BF16)] * 8,
        scratch_shapes=[
            pltpu.VMEM((4, reach, rows, cols), BF16),
            pltpu.VMEM((2, reach, heads, width, width), BF16),
            pltpu.VMEM((2, heads, width, width), BF16),
            pltpu.VMEM((reach, heads, 8, rows), F32),
            pltpu.VMEM((heads, 8, rows), F32),
            pltpu.VMEM((2, reach, 1, rows), jnp.int32),
            pltpu.VMEM((reach + 1, rows, rows), F32),
            pltpu.VMEM((reach + 1, rows, rows), F32),
            pltpu.VMEM((rows, rows), F32),
            dma((4, reach, chunks)),
            dma((4, reach, chunks)),
            dma((2, reach, chunks)),
            dma((2, reach, chunks)),
            dma((reach, chunks)),
            dma((reach, chunks)),
            dma((2, reach)),
            dma((2, reach)),
        ],
        compiler_params=pltpu.CompilerParams(
            vmem_limit_bytes=VMEM_LIMIT, collective_id=0, has_side_effects=True
        ),
        cost_estimate=pl.CostEstimate(
            flops=40 * (reach + 1) * rows * rows * cols,
            bytes_accessed=32 * rows * cols,
            transcendentals=0,
        ),
        name="attention",
    )(light_decay, ids[:, None], ids[None, :], light_q, light_k, light_v, light_grad_out, *soft)


def solution(mesh):
    wide = P(("dp", "seq"), "head")
    return jax.shard_map(
        per_device,
        mesh=mesh,
        in_specs=(P(("dp", "seq")), wide, wide, wide, P("head"), wide, wide, wide, wide, wide),
        out_specs=(wide,) * 8,
        check_vma=False,
    )
```

time: 182 us -> 154 us (0.85)
  the two profiles are of different devices: /device:TPU:24 before, /device:TPU:0 now
where the time goes in v2:
time: 154 us
  Pallas kernels  141 us (92%)
  local copies, waits for them, and re-layouts  11.6 us (8%)
    pallas_call x1, Pallas kernels, per_device(): pl.pallas_call(functools.partial(attention_kernel, shards, reach, heads,...  141 us
    unnamed x20, local copies, waits for them, and re-layouts  11.4 us

profile of v2, /device:TPU:0, one launch (start us, length us, event | category | flops | bytes accessed | tf_op | source)
XLA Modules:
  0.0 154.0 jit_solution(15616317891177402184)
XLA Ops:
  0.6 0.7 broadcast_add_fusion
  1.3 0.0 copy-start
  1.3 0.1 copy.18.ids_col
  1.5 0.5 copy-done
  2.0 141.0 %attention.1 = (bf16[256,2048]{1,0:T(8,128)(2,1)S(1)}, bf16[256,2048]{1,0:T(8,128)(2,1)S(1)}, bf16[256,2048]{1,0:T(8,128)(2,1)S(1)}, bf16[256,2048]{1,0:T(8,128)...) custom-call(f32[16]{0:T(128)S(1)} %copy-done, ...), custom_call_target="tpu_custom_call" | custom-call | flops 16106127360 | bytes 16777216 | tf_op jit(solution)/shard_map/attention/pallas_call | solution.py:388
  143.0 1.0 copy.27
  144.0 1.0 copy.28
  145.0 0.0 copy-start.5
  145.0 1.0 copy.29
  145.9 0.6 copy-done.5
  146.6 0.0 copy-start.4
  146.6 1.0 copy.30
  147.5 0.6 copy-done.4
  148.2 0.0 copy-start.3
  148.2 1.0 copy.31
  149.1 0.6 copy-done.3
  149.8 0.0 copy-start.2
  149.8 1.0 copy.32
  150.7 0.6 copy-done.2
  151.4 0.0 copy-start.1
  151.4 1.0 copy.33
  152.4 0.6 copy-done.1
  153.0 1.0 copy.34
Async XLA Ops:
  1.3 0.7 copy-start
  145.0 1.6 %copy-start.5 = (bf16[256,2048]{1,0:T(8,128)(2,1)S(1)}, bf16[256,2048]{1,0:T(8,128)(2,1)}, u32[]{:S(2)}) copy-start(bf16[256,2048]{1,0:T(8,128)(2,1)} %get-tuple-element.19) | copy-start | bytes 3145732
  146.6 1.6 %copy-start.4 = (bf16[256,2048]{1,0:T(8,128)(2,1)S(1)}, bf16[256,2048]{1,0:T(8,128)(2,1)}, u32[]{:S(2)}) copy-start(bf16[256,2048]{1,0:T(8,128)(2,1)} %get-tuple-element.20) | copy-start | bytes 3145732
  148.2 1.6 %copy-start.3 = (bf16[256,2048]{1,0:T(8,128)(2,1)S(1)}, bf16[256,2048]{1,0:T(8,128)(2,1)}, u32[]{:S(2)}) copy-start(bf16[256,2048]{1,0:T(8,128)(2,1)} %get-tuple-element.21) | copy-start | bytes 3145732
  149.8 1.6 %copy-start.2 = (bf16[256,2048]{1,0:T(8,128)(2,1)S(1)}, bf16[256,2048]{1,0:T(8,128)(2,1)}, u32[]{:S(2)}) copy-start(bf16[256,2048]{1,0:T(8,128)(2,1)} %get-tuple-element.22) | copy-start | bytes 3145732
  151.4 1.6 %copy-start.1 = (bf16[256,2048]{1,0:T(8,128)(2,1)S(1)}, bf16[256,2048]{1,0:T(8,128)(2,1)}, u32[]{:S(2)}) copy-start(bf16[256,2048]{1,0:T(8,128)(2,1)} %get-tuple-element.23) | copy-start | bytes 3145732

commit v3 on v2

--- a/solution.py
+++ b/solution.py
@@ -11,7 +11,7 @@
 NEG = -1e30
 F32 = jnp.float32
 BF16 = jnp.bfloat16
-VMEM_LIMIT = 50 * 1024 * 1024
+VMEM_LIMIT = 60 * 1024 * 1024
 
 
 def mm(a, b, ca, cb):
@@ -220,7 +220,7 @@
                 part = mm(ds, kh, 1, 0)
                 acc = part if acc is None else acc + part
             s_dq[:, cols] = (acc * scale).astype(BF16)
-            own_stats[h] = jnp.where(lane == 0, lse, delta).T[0:8, :]
+            own_stats[h] = jnp.where(lane == 0, lse, delta).T[0:2, :]
 
     def keys_side(c):
         for j in range(hb):
@@ -275,7 +275,7 @@
                 states[one, d] = jnp.zeros((heads, width, width), BF16)
                 ids_slots[one, d] = jnp.zeros((1, rows), jnp.int32)
                 if way < 0:
-                    stats[d] = jnp.zeros((heads, 8, rows), F32)
+                    stats[d] = jnp.zeros((heads, 2, rows), F32)
 
     t = lax.broadcasted_iota(jnp.int32, (rows, rows), 0)
     s = lax.broadcasted_iota(jnp.int32, (rows, rows), 1)
@@ -371,6 +371,16 @@
                     return carry
 
                 lax.fori_loop(0, chunks, drain, 0)
+
+
+def hand_out_kernel(*refs):
+    sem = refs[-1]
+    half = (len(refs) - 1) // 2
+    copies = [pltpu.make_async_copy(refs[i], refs[half + i], sem.at[i]) for i in range(half)]
+    for copy in copies:
+        copy.start()
+    for copy in copies:
+        copy.wait()
 
 
 def per_device(doc_ids, light_q, light_k, light_v, light_decay, light_grad_out, *soft):
@@ -385,7 +395,7 @@
     ids = doc_ids + 1
     vmem = pl.BlockSpec(memory_space=pltpu.VMEM)
     dma = pltpu.SemaphoreType.DMA
-    return pl.pallas_call(
+    done = pl.pallas_call(
         functools.partial(attention_kernel, shards, reach, heads, hb),
         in_specs=[pl.BlockSpec(memory_space=pltpu.SMEM)] + [vmem] * 10,
         out_specs=[vmem] * 8,
@@ -394,8 +404,8 @@
             pltpu.VMEM((4, reach, rows, cols), BF16),
             pltpu.VMEM((2, reach, heads, width, width), BF16),
             pltpu.VMEM((2, heads, width, width), BF16),
-            pltpu.VMEM((reach, heads, 8, rows), F32),
-            pltpu.VMEM((heads, 8, rows), F32),
+            pltpu.VMEM((reach, heads, 2, rows), F32),
+            pltpu.VMEM((heads, 2, rows), F32),
             pltpu.VMEM((2, reach, 1, rows), jnp.int32),
             pltpu.VMEM((reach + 1, rows, rows), F32),
             pltpu.VMEM((reach + 1, rows, rows), F32),
@@ -419,6 +429,18 @@
         ),
         name="attention",
     )(light_decay, ids[:, None], ids[None, :], light_q, light_k, light_v, light_grad_out, *soft)
+    anywhere = pl.BlockSpec(memory_space=pl.ANY)
+    return pl.pallas_call(
+        hand_out_kernel,
+        in_specs=[anywhere] * 8,
+        out_specs=[anywhere] * 8,
+        out_shape=[jax.ShapeDtypeStruct((rows, cols), BF16)] * 8,
+        scratch_shapes=[dma((8,))],
+        cost_estimate=pl.CostEstimate(
+            flops=0, bytes_accessed=32 * rows * cols, transcendentals=0
+        ),
+        name="hand_out",
+    )(*done)
 
 
 def solution(mesh):

time: 154 us -> 397 us (2.58)
  Pallas kernels: 141 us -> 394 us
  local copies, waits for them, and re-layouts: 11.6 us -> 1.36 us
    pallas_call x0 -> x1, Pallas kernels: none -> 255 us  [per_device(): pl.pallas_call(hand_out_kernel, in_specs=[anywhere] * 8, out_specs=[anywh...]
    unnamed x20 -> x2, local copies, waits for them, and re-layouts: 11.4 us -> 0.56 us
where the time goes in v3:
time: 397 us
  Pallas kernels  394 us (99%)
    pallas_call x1, Pallas kernels, per_device(): pl.pallas_call(hand_out_kernel, in_specs=[anywhere] * 8, out_specs=[anywh...  255 us
    pallas_call x1, Pallas kernels, per_device(): pl.pallas_call(functools.partial(attention_kernel, shards, reach, heads,...  139 us

profile of v3, /device:TPU:0, one launch (start us, length us, event | category | flops | bytes accessed | tf_op | source)
XLA Modules:
  0.0 396.8 jit_solution(564276272916225208)
XLA Ops:
  0.6 0.7 broadcast_add_fusion
  1.3 0.0 copy-start
  1.3 0.6 copy-done
  1.9 0.8 copy.18.ids_col
  2.7 138.9 %attention.1 = (bf16[256,2048]{1,0:T(8,128)(2,1)}, bf16[256,2048]{1,0:T(8,128)(2,1)}, bf16[256,2048]{1,0:T(8,128)(2,1)}, bf16[256,2048]{1,0:T(8,128)(2,1)}, bf16...) custom-call(f32[16]{0:T(128)} %decay.1, ...), custom_call_target="tpu_custom_call" | custom-call | flops 16106127360 | bytes 16777216 | tf_op jit(solution)/shard_map/attention/pallas_call | solution.py:398
  141.5 255.3 %hand_out.1 = (bf16[256,2048]{1,0:T(8,128)(2,1)}, bf16[256,2048]{1,0:T(8,128)(2,1)}, bf16[256,2048]{1,0:T(8,128)(2,1)}, bf16[256,2048]{1,0:T(8,128)(2,1)}, bf16[...) custom-call(bf16[256,2048]{1,0:T(8,128)(2,1)} %get-tuple-element.16.ref, ...), custom_call_target="tpu_custom_call" | custom-call | bytes 16777216 | tf_op jit(solution)/shard_map/hand_out/pallas_call | solution.py:433
Async XLA Ops:
  1.3 0.6 copy-start

commit v4 on v3

--- a/solution.py
+++ b/solution.py
@@ -374,13 +374,9 @@
 
 
 def hand_out_kernel(*refs):
-    sem = refs[-1]
-    half = (len(refs) - 1) // 2
-    copies = [pltpu.make_async_copy(refs[i], refs[half + i], sem.at[i]) for i in range(half)]
-    for copy in copies:
-        copy.start()
-    for copy in copies:
-        copy.wait()
+    half = len(refs) // 2
+    for i in range(half):
+        refs[half + i][...] = refs[i][...]
 
 
 def per_device(doc_ids, light_q, light_k, light_v, light_decay, light_grad_out, *soft):
@@ -429,13 +425,14 @@
         ),
         name="attention",
     )(light_decay, ids[:, None], ids[None, :], light_q, light_k, light_v, light_grad_out, *soft)
-    anywhere = pl.BlockSpec(memory_space=pl.ANY)
+    piece = pl.BlockSpec((rows // 4, cols), lambda i: (i, 0))
     return pl.pallas_call(
         hand_out_kernel,
-        in_specs=[anywhere] * 8,
-        out_specs=[anywhere] * 8,
+        grid=(4,),
+        in_specs=[piece] * 8,
+        out_specs=[piece] * 8,
         out_shape=[jax.ShapeDtypeStruct((rows, cols), BF16)] * 8,
-        scratch_shapes=[dma((8,))],
+        compiler_params=pltpu.CompilerParams(vmem_limit_bytes=VMEM_LIMIT),
         cost_estimate=pl.CostEstimate(
             flops=0, bytes_accessed=32 * rows * cols, transcendentals=0
         ),

time: 397 us -> 149 us (0.38)
  Pallas kernels: 394 us -> 146 us
    pallas_call x1, Pallas kernels: 255 us -> 6.94 us  [per_device(): pl.pallas_call(hand_out_kernel, grid=(4,), in_specs=[piece] * 8, out_spec...]
where the time goes in v4:
time: 149 us; the launch traced here: 148 us
  Pallas kernels  146 us (98%)
    pallas_call x1, Pallas kernels, per_device(): pl.pallas_call(functools.partial(attention_kernel, shards, reach, heads,...  139 us
    pallas_call x1, Pallas kernels, per_device(): pl.pallas_call(hand_out_kernel, grid=(4,), in_specs=[piece] * 8, out_spec...  6.94 us

profile of v4, /device:TPU:0, one launch (start us, length us, event | category | flops | bytes accessed | tf_op | source)
XLA Modules:
  0.0 148.5 jit_solution(16377186963698017723)
XLA Ops:
  0.6 0.7 broadcast_add_fusion
  1.3 0.0 copy-start
  1.3 0.6 copy-done
  1.9 0.8 copy.18.ids_col
  2.7 138.9 %attention.1 = (bf16[256,2048]{1,0:T(8,128)(2,1)}, bf16[256,2048]{1,0:T(8,128)(2,1)}, bf16[256,2048]{1,0:T(8,128)(2,1)}, bf16[256,2048]{1,0:T(8,128)(2,1)}, bf16...) custom-call(f32[16]{0:T(128)} %decay.1, ...), custom_call_target="tpu_custom_call" | custom-call | flops 16106127360 | bytes 16777216 | tf_op jit(solution)/shard_map/attention/pallas_call | solution.py:394
  141.5 6.9 %hand_out.1 = (bf16[256,2048]{1,0:T(8,128)(2,1)}, bf16[256,2048]{1,0:T(8,128)(2,1)}, bf16[256,2048]{1,0:T(8,128)(2,1)}, bf16[256,2048]{1,0:T(8,128)(2,1)}, bf16[...) custom-call(bf16[256,2048]{1,0:T(8,128)(2,1)} %get-tuple-element.16.ref, ...), custom_call_target="tpu_custom_call" | custom-call | bytes 16777216 | tf_op jit(solution)/shard_map/hand_out/pallas_call | solution.py:429
Async XLA Ops:
  1.3 0.6 copy-start
